TPU v7x, 32 devices: a whole 2x2x4 slice. The times are simulated.
32 devices in a mesh: dp: 16 (over z, y, x), mp: 2 (over core).
Axes of the slice: x: 2, y: 2, z: 4, core: 2. Of those that a mesh axis runs over, the one named last changes fastest.
Arguments:
- token_ids: int32 [32, 1024], P('dp'), may hold values from 0 to 820
- segment_ids: int32 [32, 1024], P('dp'), may hold values from 0 to 15, never falling along the last dimension, each value on 1 to 128 neighbouring positions
- timesteps: int32 [32], P('dp'), may hold values from 0 to 1999
- noise: float32 [32, 1024, 128], P('dp'), may hold values from -6 to 6
- bucket_ids: int32 [32, 1024], P('dp'), may hold values from 0 to 15, as said below
- counted: int32 [32, 1024], P('dp'), may hold values from 0 to 1, as said below
- embed: float32 [821, 128], replicated, may hold values from -0.9 to 0.9
- up_weight: float32 [128, 768], replicated, may hold values from -0.5 to 0.5
- down_weight: float32 [768, 128], replicated, may hold values from -0.21875 to 0.21875
- qkv_weight: float32 [3, 768, 768], P(None, 'dp', 'mp'), may hold values from -0.21875 to 0.21875
- out_weight: float32 [768, 768], P('mp', 'dp'), may hold values from -0.625 to 0.625
- fc_weight: float32 [768, 3072], P('dp', 'mp'), may hold values from -0.21875 to 0.21875
- proj_weight: float32 [3072, 768], P('mp', 'dp'), may hold values from -0.109375 to 0.109375
- norm_params: float32 [6, 768], replicated, as said below
- embed_m: float32 [821, 128], replicated, may hold values from -2.3841858e-06 to 2.3841858e-06
- embed_v: float32 [821, 128], replicated, may hold values from 1.3542443e-14 to 5.4169773e-14
- up_m: float32 [128, 768], replicated, may hold values from -2.3841858e-06 to 2.3841858e-06
- up_v: float32 [128, 768], replicated, may hold values from 1.3542443e-14 to 5.4169773e-14
- down_m: float32 [768, 128], replicated, may hold values from -2.3841858e-06 to 2.3841858e-06
- down_v: float32 [768, 128], replicated, may hold values from 1.3542443e-14 to 5.4169773e-14
- qkv_m: float32 [3, 768, 768], P(None, 'dp', 'mp'), may hold values from -2.3841858e-06 to 2.3841858e-06
- qkv_v: float32 [3, 768, 768], P(None, 'dp', 'mp'), may hold values from 1.3542443e-14 to 5.4169773e-14
- out_m: float32 [768, 768], P('mp', 'dp'), may hold values from -2.3841858e-06 to 2.3841858e-06
- out_v: float32 [768, 768], P('mp', 'dp'), may hold values from 1.3542443e-14 to 5.4169773e-14
- fc_m: float32 [768, 3072], P('dp', 'mp'), may hold values from -2.3841858e-06 to 2.3841858e-06
- fc_v: float32 [768, 3072], P('dp', 'mp'), may hold values from 1.3542443e-14 to 5.4169773e-14
- proj_m: float32 [3072, 768], P('mp', 'dp'), may hold values from -2.3841858e-06 to 2.3841858e-06
- proj_v: float32 [3072, 768], P('mp', 'dp'), may hold values from 1.3542443e-14 to 5.4169773e-14
- norm_m: float32 [6, 768], replicated, may hold values from -2.2888184e-05 to 2.2888184e-05
- norm_v: float32 [6, 768], replicated, may hold values from 1.3542443e-12 to 5.416977e-12
Outputs:
- loss_sum: float32 [], replicated
- weight_total: float32 [], replicated
- grad_norm: float32 [], replicated
- embed_first: float32 [821, 128], replicated
- embed_second: float32 [821, 128], replicated
- embed_next: float32 [821, 128], replicated
- up_first: float32 [128, 768], replicated
- up_second: float32 [128, 768], replicated
- up_next: float32 [128, 768], replicated
- down_first: float32 [768, 128], replicated
- down_second: float32 [768, 128], replicated
- down_next: float32 [768, 128], replicated
- qkv_first: float32 [3, 768, 768], P(None, 'dp', 'mp')
- qkv_second: float32 [3, 768, 768], P(None, 'dp', 'mp')
- qkv_next: float32 [3, 768, 768], P(None, 'dp', 'mp')
- out_first: float32 [768, 768], P('mp', 'dp')
- out_second: float32 [768, 768], P('mp', 'dp')
- out_next: float32 [768, 768], P('mp', 'dp')
- fc_first: float32 [768, 3072], P('dp', 'mp')
- fc_second: float32 [768, 3072], P('dp', 'mp')
- fc_next: float32 [768, 3072], P('dp', 'mp')
- proj_first: float32 [3072, 768], P('mp', 'dp')
- proj_second: float32 [3072, 768], P('mp', 'dp')
- proj_next: float32 [3072, 768], P('mp', 'dp')
- norm_first: float32 [6, 768], replicated
- norm_second: float32 [6, 768], replicated
- norm_next: float32 [6, 768], replicated
Inputs may be any that keep to these rules, and one draw needn't show every extreme that they name: `counted`: 1 marks a position whose loss counts. `bucket_ids`: one bucket, which differs from draw to draw, holds no position. `norm_params`: rows 0, 2 and 4 hold the gains and rows 1, 3 and 5 the shifts of the three norms.
All inputs are finite; a program needn't handle non-finite values.
Results may differ from a plain program's by a relative error of at most 0.0075.
Values may be sent and summed in bfloat16 or wider, within the bound.
A program may use at most 320 MiB of HBM per device.

v0:
```python
import math

import jax
import jax.numpy as jnp
from jax import lax
from jax.sharding import PartitionSpec as P

HEAD_DIM = 64
NB = 16
T_STEPS = 2000
STEP = 10


NORM_EPS = 1e-05
MASKED = -1e30
BETA_FIRST = 0.9
BETA_SECOND = 0.999
ADAM_EPS = 1e-08
MATRIX_RATE = 0.05
NORM_RATE = 0.5
WEIGHT_DECAY = 0.1
CLIP_NORM = 0.01
BLOCK_ROWS = 512


def layer_norm(values, gain, shift):
    center = values - jnp.mean(values, axis=-1, keepdims=True)
    spread = jnp.mean(center * center, axis=-1, keepdims=True)
    return center * lax.rsqrt(spread + NORM_EPS) * gain + shift


def norm_back(values, gain, shift, upstream):
    unused, pull = jax.vjp(layer_norm, values, gain, shift)
    return pull(upstream)


def gelu_back(inputs, upstream):
    unused, pull = jax.vjp(jax.nn.gelu, inputs)
    return pull(upstream)[0]


def sinusoid(where, width):
    half = width // 2
    freqs = jnp.exp(-math.log(10000.0) * jnp.arange(half, dtype=jnp.float32) / half)
    angles = where[:, None] * freqs[None, :]
    return jnp.concatenate([jnp.sin(angles), jnp.cos(angles)], axis=-1)


def product(left, right):
    return jnp.dot(left, right, preferred_element_type=jnp.float32)


def product_tn(left, right):
    return lax.dot_general(
        left, right, (((0,), (0,)), ((), ())), preferred_element_type=jnp.float32
    )


def product_nt(left, right):
    return lax.dot_general(
        left, right, (((1,), (1,)), ((), ())), preferred_element_type=jnp.float32
    )


def combine_sum(partial_sum):
    shares = lax.psum_scatter(
        partial_sum.astype(jnp.bfloat16), "mp", scatter_dimension=0, tiled=True
    ).astype(jnp.float32)
    return lax.all_gather(shares.astype(jnp.bfloat16), "mp", axis=0, tiled=True).astype(
        shares.dtype
    )


def block_scores(query_block, keys_all, segment_block, segment_all):
    scale = query_block.shape[-1] ** (-0.5)
    scores = (
        jnp.einsum("qhd,khd->hqk", query_block, keys_all, preferred_element_type=jnp.float32)
        * scale
    )
    same = segment_block[:, None] == segment_all[None, :]
    return jnp.where(same[None], scores, MASKED)


def attend_forward(queries, keys_all, values_all, segments):
    length = queries.shape[0]
    block = min(BLOCK_ROWS, length)
    results = []
    totals = []
    for first in range(0, length, block):
        scores = block_scores(
            queries[first : first + block], keys_all, segments[first : first + block], segments
        )
        log_total = jax.nn.logsumexp(scores, axis=-1)
        probs = jnp.exp(scores - log_total[..., None]).astype(jnp.bfloat16)
        results.append(
            jnp.einsum("hqk,khd->qhd", probs, values_all, preferred_element_type=jnp.float32)
        )
        totals.append(log_total)
    return (jnp.concatenate(results, axis=0), jnp.concatenate(totals, axis=1))


def attend_backward(queries, keys_all, values_all, segments, log_total, upstream):
    length = queries.shape[0]
    block = min(BLOCK_ROWS, length)
    scale = queries.shape[-1] ** (-0.5)
    grad_keys = jnp.zeros(keys_all.shape, jnp.float32)
    grad_values = jnp.zeros(values_all.shape, jnp.float32)
    grad_queries = []
    for first in range(0, length, block):
        query_block = queries[first : first + block]
        up_block = upstream[first : first + block]
        scores = block_scores(query_block, keys_all, segments[first : first + block], segments)
        probs = jnp.exp(scores - log_total[:, first : first + block, None])
        grad_values = grad_values + jnp.einsum(
            "hqk,qhd->khd", probs.astype(jnp.bfloat16), up_block, preferred_element_type=jnp.float32
        )
        grad_probs = jnp.einsum(
            "qhd,khd->hqk", up_block, values_all, preferred_element_type=jnp.float32
        )
        inner = jnp.sum(grad_probs * probs, axis=-1, keepdims=True)
        grad_scores = (probs * (grad_probs - inner)).astype(jnp.bfloat16)
        grad_queries.append(
            jnp.einsum("hqk,khd->qhd", grad_scores, keys_all, preferred_element_type=jnp.float32)
            * scale
        )
        grad_keys = (
            grad_keys
            + jnp.einsum(
                "hqk,qhd->khd", grad_scores, query_block, preferred_element_type=jnp.float32
            )
            * scale
        )
    return (jnp.concatenate(grad_queries, axis=0), grad_keys, grad_values)


def layer_forward(token_row, segment_row, timestep, noise_row, small, layer):
    embed, up_low, down_low, norms = small
    qkv_low, out_low, fc_low, proj_low = layer
    length = token_row.shape[0]
    width = up_low.shape[1]
    start = jnp.take(embed, token_row, axis=0)
    keep = 1.0 - jnp.sqrt(timestep.astype(jnp.float32) / T_STEPS + 0.0001)
    noisy_low = (jnp.sqrt(keep) * start + jnp.sqrt(1.0 - keep) * noise_row).astype(jnp.bfloat16)
    places = sinusoid(jnp.arange(length, dtype=jnp.float32), width) + sinusoid(
        timestep.astype(jnp.float32).reshape(1), width
    )
    hidden_zero = product(noisy_low, up_low) + places
    normed_one = layer_norm(hidden_zero, norms[0], norms[1]).astype(jnp.bfloat16)
    projected = jnp.einsum(
        "ld,jde->jle", normed_one, qkv_low, preferred_element_type=jnp.float32
    ).astype(jnp.bfloat16)
    heads = projected.reshape(3, length, -1, HEAD_DIM)
    attended, log_total = attend_forward(heads[0], heads[1], heads[2], segment_row)
    attended = attended.reshape(length, -1).astype(jnp.bfloat16)
    hidden_one = hidden_zero + combine_sum(product(attended, out_low))
    normed_two = layer_norm(hidden_one, norms[2], norms[3]).astype(jnp.bfloat16)
    pre_act = product(normed_two, fc_low)
    activated = jax.nn.gelu(pre_act).astype(jnp.bfloat16)
    hidden_two = hidden_one + combine_sum(product(activated, proj_low))
    normed_end = layer_norm(hidden_two, norms[4], norms[5]).astype(jnp.bfloat16)
    predicted = product(normed_end, down_low)
    return (
        start,
        keep,
        noisy_low,
        hidden_zero,
        normed_one,
        heads,
        log_total,
        attended,
        hidden_one,
        normed_two,
        pre_act,
        activated,
        hidden_two,
        normed_end,
        predicted,
    )


def layer_backward(token_row, segment_row, scale_row, weight_total, saved, small, embed_low, layer):
    embed, up_low, down_low, norms = small
    qkv_low, out_low, fc_low, proj_low = layer
    (
        start,
        keep,
        noisy_low,
        hidden_zero,
        normed_one,
        heads,
        log_total,
        attended,
        hidden_one,
        normed_two,
        pre_act,
        activated,
        hidden_two,
        normed_end,
        predicted,
    ) = saved
    length, emb_width = predicted.shape
    vocab = embed.shape[0]
    pred_low = predicted.astype(jnp.bfloat16)
    logits = product_nt(pred_low, embed_low)
    log_norm = jax.nn.logsumexp(logits, axis=-1)
    onehot = (token_row[:, None] == jnp.arange(vocab)[None, :]).astype(jnp.float32)
    picked = jnp.sum(logits * onehot, axis=-1)
    error = predicted - start
    per_token = jnp.sum(error * error, axis=-1) / emb_width + log_norm - picked
    loss_part = jnp.sum(scale_row * per_token)
    weighting = scale_row / weight_total
    grad_logits = (weighting[:, None] * (jnp.exp(logits - log_norm[:, None]) - onehot)).astype(
        jnp.bfloat16
    )
    grad_error = weighting[:, None] * 2.0 * error / emb_width
    grad_pred = (product(grad_logits, embed_low) + grad_error).astype(jnp.bfloat16)
    grad_down = product_tn(normed_end, grad_pred)
    grad_two, gain_grad_end, shift_grad_end = norm_back(
        hidden_two, norms[4], norms[5], product_nt(grad_pred, down_low)
    )
    branch_two = grad_two.astype(jnp.bfloat16)
    grad_proj = product_tn(activated, branch_two)
    grad_pre = gelu_back(pre_act, product_nt(branch_two, proj_low)).astype(jnp.bfloat16)
    grad_fc = product_tn(normed_two, grad_pre)
    back_two, gain_grad_mid, shift_grad_mid = norm_back(
        hidden_one, norms[2], norms[3], combine_sum(product_nt(grad_pre, fc_low))
    )
    grad_one = grad_two + back_two
    branch_one = grad_one.astype(jnp.bfloat16)
    grad_out = product_tn(attended, branch_one)
    grad_att = product_nt(branch_one, out_low).astype(jnp.bfloat16).reshape(length, -1, HEAD_DIM)
    grad_query, grad_key, grad_value = attend_backward(
        heads[0], heads[1], heads[2], segment_row, log_total, grad_att
    )
    grad_heads = (
        jnp.stack([grad_query, grad_key, grad_value]).reshape(3, length, -1).astype(jnp.bfloat16)
    )
    grad_qkv = jnp.einsum("ld,jle->jde", normed_one, grad_heads, preferred_element_type=jnp.float32)
    back_input = jnp.einsum("jle,jde->ld", grad_heads, qkv_low, preferred_element_type=jnp.float32)
    back_one, gain_grad_first, shift_grad_first = norm_back(
        hidden_zero, norms[0], norms[1], combine_sum(back_input)
    )
    grad_zero = (grad_one + back_one).astype(jnp.bfloat16)
    grad_up = product_tn(noisy_low, grad_zero)
    grad_start = jnp.sqrt(keep) * product_nt(grad_zero, up_low) - grad_error
    lookup_grad = lax.dot_general(
        onehot,
        grad_start,
        (((0,), (0,)), ((), ())),
        precision=lax.Precision.HIGHEST,
        preferred_element_type=jnp.float32,
    )
    grad_embed = product_tn(grad_logits, pred_low) + lookup_grad
    grad_norms = jnp.stack(
        [
            gain_grad_first,
            shift_grad_first,
            gain_grad_mid,
            shift_grad_mid,
            gain_grad_end,
            shift_grad_end,
        ]
    )
    return (
        loss_part,
        (grad_qkv, grad_out, grad_fc, grad_proj),
        (grad_embed, grad_up, grad_down, grad_norms),
    )


def adam_update(weight, grad, first, second, rate, decay):
    first_new = BETA_FIRST * first + (1.0 - BETA_FIRST) * grad
    second_new = BETA_SECOND * second + (1.0 - BETA_SECOND) * grad * grad
    first_hat = first_new / (1.0 - BETA_FIRST**STEP)
    second_hat = second_new / (1.0 - BETA_SECOND**STEP)
    weight_new = weight - rate * (first_hat / (jnp.sqrt(second_hat) + ADAM_EPS) + decay * weight)
    return (first_new, second_new, weight_new)


def per_device(
    token_ids,
    segment_ids,
    timesteps,
    noise,
    bucket_ids,
    counted,
    embed,
    up_weight,
    down_weight,
    qkv_weight,
    out_weight,
    fc_weight,
    proj_weight,
    norm_params,
    embed_m,
    embed_v,
    up_m,
    up_v,
    down_m,
    down_v,
    qkv_m,
    qkv_v,
    out_m,
    out_v,
    fc_m,
    fc_v,
    proj_m,
    proj_v,
    norm_m,
    norm_v,
):
    micro_count = token_ids.shape[0]
    live = counted.astype(jnp.float32)
    bucket_hot = (bucket_ids[..., None] == jnp.arange(NB)[None, None, :]).astype(jnp.float32)
    counts = lax.psum(jnp.sum(live[..., None] * bucket_hot, axis=(0, 1)), "dp")
    live_total = jnp.sum(counts)
    bucket_weight = live_total / (NB * jnp.maximum(counts, 1.0))
    weight_total = jnp.sum(counts * bucket_weight)
    token_scale = live * jnp.sum(bucket_hot * bucket_weight, axis=-1)
    token_rows, segment_rows, time_rows, noise_rows, scale_rows = (
        token_ids,
        segment_ids,
        timesteps,
        noise,
        token_scale,
    )
    small = (embed, up_weight.astype(jnp.bfloat16), down_weight.astype(jnp.bfloat16), norm_params)
    embed_low = embed.astype(jnp.bfloat16)
    qkv_local = qkv_weight.astype(jnp.bfloat16)
    out_local = out_weight.astype(jnp.bfloat16)
    fc_local = fc_weight.astype(jnp.bfloat16)
    proj_local = proj_weight.astype(jnp.bfloat16)
    layer_total = None
    small_total = None
    loss_total = jnp.zeros((), jnp.float32)
    for micro_index in range(micro_count):
        layer = (
            lax.all_gather(qkv_local, "dp", axis=1, tiled=True),
            lax.all_gather(out_local, "dp", axis=1, tiled=True),
            lax.all_gather(fc_local, "dp", axis=0, tiled=True),
            lax.all_gather(proj_local, "dp", axis=1, tiled=True),
        )
        saved = layer_forward(
            token_rows[micro_index],
            segment_rows[micro_index],
            time_rows[micro_index],
            noise_rows[micro_index],
            small,
            layer,
        )
        back_layer = (
            lax.all_gather(qkv_local, "dp", axis=1, tiled=True),
            lax.all_gather(out_local, "dp", axis=1, tiled=True),
            lax.all_gather(fc_local, "dp", axis=0, tiled=True),
            lax.all_gather(proj_local, "dp", axis=1, tiled=True),
        )
        loss_part, layer_grads, small_grads = layer_backward(
            token_rows[micro_index],
            segment_rows[micro_index],
            scale_rows[micro_index],
            weight_total,
            saved,
            small,
            embed_low,
            back_layer,
        )
        layer_total = (
            layer_grads
            if layer_total is None
            else tuple((earlier + later for earlier, later in zip(layer_total, layer_grads)))
        )
        small_total = (
            small_grads
            if small_total is None
            else tuple((earlier + later for earlier, later in zip(small_total, small_grads)))
        )
        loss_total = loss_total + loss_part
    layer_shards = (
        lax.psum_scatter(layer_total[0], "dp", scatter_dimension=1, tiled=True),
        lax.psum_scatter(layer_total[1], "dp", scatter_dimension=1, tiled=True),
        lax.psum_scatter(layer_total[2], "dp", scatter_dimension=0, tiled=True),
        lax.psum_scatter(layer_total[3], "dp", scatter_dimension=1, tiled=True),
    )
    grad_embed, grad_up, grad_down, grad_norms, loss_sum = lax.psum(
        (small_total[0], small_total[1], small_total[2], small_total[3], loss_total), "dp"
    )
    local_squares = sum((jnp.sum(piece * piece) for piece in layer_shards))
    block_squares = lax.psum(local_squares, ("dp", "mp"))
    small_squares = sum(
        (jnp.sum(piece * piece) for piece in (grad_embed, grad_up, grad_down, grad_norms))
    )
    grad_norm = jnp.sqrt(block_squares + small_squares)
    factor = jnp.minimum(1.0, CLIP_NORM / (grad_norm + 1e-06))
    embed_first, embed_second, embed_next = adam_update(
        embed, factor * grad_embed, embed_m, embed_v, MATRIX_RATE, WEIGHT_DECAY
    )
    up_first, up_second, up_next = adam_update(
        up_weight, factor * grad_up, up_m, up_v, MATRIX_RATE, WEIGHT_DECAY
    )
    down_first, down_second, down_next = adam_update(
        down_weight, factor * grad_down, down_m, down_v, MATRIX_RATE, WEIGHT_DECAY
    )
    qkv_first, qkv_second, qkv_next = adam_update(
        qkv_weight, factor * layer_shards[0], qkv_m, qkv_v, MATRIX_RATE, WEIGHT_DECAY
    )
    out_first, out_second, out_next = adam_update(
        out_weight, factor * layer_shards[1], out_m, out_v, MATRIX_RATE, WEIGHT_DECAY
    )
    fc_first, fc_second, fc_next = adam_update(
        fc_weight, factor * layer_shards[2], fc_m, fc_v, MATRIX_RATE, WEIGHT_DECAY
    )
    proj_first, proj_second, proj_next = adam_update(
        proj_weight, factor * layer_shards[3], proj_m, proj_v, MATRIX_RATE, WEIGHT_DECAY
    )
    norm_first, norm_second, norm_next = adam_update(
        norm_params, factor * grad_norms, norm_m, norm_v, NORM_RATE, 0.0
    )
    return (
        loss_sum,
        weight_total,
        grad_norm,
        embed_first,
        embed_second,
        embed_next,
        up_first,
        up_second,
        up_next,
        down_first,
        down_second,
        down_next,
        qkv_first,
        qkv_second,
        qkv_next,
        out_first,
        out_second,
        out_next,
        fc_first,
        fc_second,
        fc_next,
        proj_first,
        proj_second,
        proj_next,
        norm_first,
        norm_second,
        norm_next,
    )


def solution(mesh):
    placed = (
        P("dp", None),
        P("dp", None),
        P("dp"),
        P("dp", None, None),
        P("dp", None),
        P("dp", None),
        P(),
        P(),
        P(),
        P(None, "dp", "mp"),
        P("mp", "dp"),
        P("dp", "mp"),
        P("mp", "dp"),
        P(),
        P(),
        P(),
        P(),
        P(),
        P(),
        P(),
        P(None, "dp", "mp"),
        P(None, "dp", "mp"),
        P("mp", "dp"),
        P("mp", "dp"),
        P("dp", "mp"),
        P("dp", "mp"),
        P("mp", "dp"),
        P("mp", "dp"),
        P(),
        P(),
    )
    return jax.shard_map(
        per_device,
        mesh=mesh,
        in_specs=placed,
        out_specs=(
            P(),
            P(),
            P(),
            P(),
            P(),
            P(),
            P(),
            P(),
            P(),
            P(),
            P(),
            P(),
            P(None, "dp", "mp"),
            P(None, "dp", "mp"),
            P(None, "dp", "mp"),
            P("mp", "dp"),
            P("mp", "dp"),
            P("mp", "dp"),
            P("dp", "mp"),
            P("dp", "mp"),
            P("dp", "mp"),
            P("mp", "dp"),
            P("mp", "dp"),
            P("mp", "dp"),
            P(),
            P(),
            P(),
        ),
        check_vma=False,
    )
```

profile of v0, /device:TPU:0, one launch (start us, length us, event | category | flops | bytes accessed | tf_op | source)
XLA Modules:
  0.0 1377.9 jit_solution(13940810429717392590)
XLA Ops:
  40.4 49.9 %all_gather.49 = bf16[384,768]{0,1:T(8,128)(2,1)} all-gather(bf16[384,48]{0,1:T(8,128)(2,1)S(1)} %convert_element_type.249), channel_id=1, replica_groups=mesh['dp'=16,'mp'=2] {'dp'}, dimensions={1}, use_global_device_ids=true | all-gather | bytes 626688 | tf_op jit(solution)/shard_map/all_gather | solution.py:339
  118.4 7.9 fusion.55
  146.2 7.9 fusion.57
  162.7 12.1 all-gather.14.cloned.1.call-done
  180.0 61.6 %all-gather.16.cloned.1.call-done = bf16[768,1536]{1,0:T(8,128)(2,1)} async-done(((bf16[48,1536]{1,0:T(8,128)(2,1)}), bf16[768,1536]{1,0:T(8,128)(2,1)}) %all-gather.16.cloned.1.call-update) | async-done | bytes 2359312 | tf_op jit(solution)/shard_map/all_gather | solution.py:340
  241.6 8.1 fusion.120
  249.6 56.3 %all-gather.18.cloned.1.call-done = bf16[1536,768]{0,1:T(8,128)(2,1)} async-done(((bf16[1536,48]{0,1:T(8,128)(2,1)}), bf16[1536,768]{0,1:T(8,128)(2,1)}) %all-gather.18.cloned.1.call-update) | async-done | bytes 2359312 | tf_op jit(solution)/shard_map/all_gather | solution.py:341
  305.9 7.4 convolution_convert_fusion.5
  332.8 42.0 %psum.49 = f32[16]{0:T(128)S(1)} all-reduce(f32[16]{0:T(128)S(1)} %select_reduce_fusion.3), channel_id=1, replica_groups=mesh['dp'=16,'mp'=2] {'dp'}, use_global_device_ids=true, to_apply=%region_1.0 | all-reduce | flops 16 | bytes 128 | tf_op jit(solution)/shard_map/psum | solution.py:315
  413.7 7.1 multiply_reduce_fusion.4
  437.6 9.4 reduce-scatter.22.cloned.1.call-done
  447.3 12.4 all-gather.28.cloned.1.call-done
  476.4 8.0 multiply_reduce_fusion.1
  484.5 10.7 multiply_convert_fusion.1
  504.1 7.6 multiply_reduce_fusion
  515.3 7.2 multiply_convert_fusion
  530.3 9.7 fusion.14
  546.0 9.8 reduce-scatter.20.cloned.1.call-done
  555.9 12.4 all-gather.32.cloned.1.call-done
  580.8 9.7 convert_reduce_fusion.3
  600.6 7.7 multiply_reduce_fusion.3
  608.3 11.0 multiply_convert_fusion.3
  628.4 7.6 multiply_reduce_fusion.2
  640.6 6.9 multiply_convert_fusion.2
  655.3 10.3 reduce-scatter.30.cloned.1.call-done
  672.2 8.0 convolution_add_fusion
  743.3 78.6 %reduce-scatter.28.cloned.1.call-done = f32[1536,48]{0,1:T(8,128)} async-done(((f32[1536,768]{0,1:T(8,128)}), f32[1536,48]{0,1:T(8,128)}) %reduce-scatter.28.cloned.1.call-update) | async-done | bytes 294928 | tf_op jit(solution)/shard_map/reduce_scatter | solution.py:382
  823.5 141.1 %reduce-scatter.26.cloned.1.call-done = f32[48,1536]{1,0:T(8,128)} async-done(((f32[768,1536]{1,0:T(8,128)}), f32[48,1536]{1,0:T(8,128)}) %reduce-scatter.26.cloned.1.call-update) | async-done | bytes 294928 | tf_op jit(solution)/shard_map/reduce_scatter | solution.py:381
  966.5 126.4 %reduce-scatter.24.cloned.1.call-done = f32[384,48]{0,1:T(8,128)} async-done(((f32[384,768]{0,1:T(8,128)}), f32[384,48]{0,1:T(8,128)}) %reduce-scatter.24.cloned.1.call-update) | async-done | bytes 73744 | tf_op jit(solution)/shard_map/reduce_scatter | solution.py:380
  1094.4 77.9 %all-reduce.1 = (f32[]{:T(128)}, f32[6,768]{1,0:T(8,128)S(1)}) all-reduce(f32[]{:T(128)S(6)} %add.544, f32[6,768]{1,0:T(8,128)S(1)} %add.574), channel_id=1, replica_groups=mesh['dp'=16,'mp'=2] {'dp'}, use_global_device_ids=true, to_apply=%region_38.40 | all-reduce | flops 4609 | bytes 36872 | tf_op jit(solution)/shard_map/psum | solution.py:384
  1172.9 133.9 %all-reduce.5.cloned.1.call-done = (f32[3,768,384]{2,0,1:T(4,128)}, f32[821,128]{1,0:T(8,128)}, f32[128,768]{1,0:T(8,128)}, f32[768,128]{1,0:T(8,128)}) async-done(((f32[3,768,384]{2,0,1:T(4,128)}, f32[821,128]{1,0:T(8,128)}, f32[128,768]{1,0:T(8,128)}, f32[768,128]{1,0:T(8,128)}), (f32[3,768,384]{2,0,1:T(4,128)}, f32[821,128]{1,0:T(8,128)}, f32[128,768]{1,0:T(8,128)}, ...) | async-done | bytes 4745744
  1316.5 39.6 %psum.51 = f32[]{:T(128)} all-reduce(f32[]{:T(128)S(6)} %add.564), channel_id=1, replica_groups=mesh['dp'=16,'mp'=2] {'dp','mp'}, use_global_device_ids=true, to_apply=%region_62.64 | all-reduce | flops 1 | bytes 8 | tf_op jit(solution)/shard_map/psum | solution.py:388
  (692 shorter events, 343.6 us)
Async XLA Ops:
  7.2 84.4 %all-gather.12.cloned.1.call-start = ((), (), s32[]{:S(2)}) async-start(), calls=%async_computation.11 | async-start | bytes 1880064 | tf_op jit(solution)/shard_map/all_gather | solution.py:338
  8.9 148.5 %reduce-scatter.12.cloned.1.call-start = ((), (), s32[]{:S(2)}) async-start(), calls=%async_computation.12 | async-start | bytes 2359296 | tf_op jit(solution)/shard_map/reduce_scatter | solution.py:66
  12.6 384.9 %copy-start.138 = (s32[1,1024]{1,0:T(1,128)}, s32[1,1024]{1,0:T(1,128)S(1)}, u32[]{:S(2)}) copy-start(s32[1,1024]{1,0:T(1,128)S(1)} %get-tuple-element.219) | copy-start | bytes 12292
  15.8 303.8 %copy-start.177 = (f32[768]{0:T(1024)}, f32[768]{0:T(1024)S(1)}, u32[]{:S(2)}) copy-start(f32[768]{0:T(1024)S(1)} %get-tuple-element.134) | copy-start | bytes 9220
  129.5 32.9 %reduce-scatter.16.cloned.1.call-start = ((), (), s32[]{:S(2)}) async-start(), calls=%async_computation.18 | async-start | bytes 2359296 | tf_op jit(solution)/shard_map/reduce_scatter | solution.py:66
  157.3 17.5 %all-gather.14.cloned.1.call-start = ((), (), s32[]{:S(2)}) async-start(), calls=%async_computation.13 | async-start | bytes 2359296 | tf_op jit(solution)/shard_map/all_gather | solution.py:69
  157.9 83.7 %all-gather.16.cloned.1.call-start = ((), (), s32[]{:S(2)}) async-start(), calls=%async_computation.14 | async-start | bytes 2506752 | tf_op jit(solution)/shard_map/all_gather | solution.py:340
  159.6 146.3 %all-gather.18.cloned.1.call-start = ((), (), s32[]{:S(2)}) async-start(), calls=%async_computation.15 | async-start | bytes 2506752 | tf_op jit(solution)/shard_map/all_gather | solution.py:341
  161.3 154.8 %all-gather.22.cloned.1.call-start = ((), (), s32[]{:S(2)}) async-start(), calls=%async_computation.19 | async-start | bytes 2359296 | tf_op jit(solution)/shard_map/all_gather | solution.py:69
  162.4 169.2 %reduce-scatter.14.cloned.1.call-start = ((), (), s32[]{:S(2)}) async-start(), calls=%async_computation.16 | async-start | bytes 2359296 | tf_op jit(solution)/shard_map/reduce_scatter | solution.py:66
  313.3 63.2 %reduce-scatter.18.cloned.1.call-start = ((), (), s32[]{:S(2)}) async-start(), calls=%async_computation.20 | async-start | bytes 2359296 | tf_op jit(solution)/shard_map/reduce_scatter | solution.py:66
  331.6 46.3 %all-gather.20.cloned.1.call-start = ((), (), s32[]{:S(2)}) async-start(), calls=%async_computation.17 | async-start | bytes 2359296 | tf_op jit(solution)/shard_map/all_gather | solution.py:69
  332.1 51.2 %all-gather.24.cloned.1.call-start = ((), (), s32[]{:S(2)}) async-start(), calls=%async_computation.21 | async-start | bytes 2359296 | tf_op jit(solution)/shard_map/all_gather | solution.py:69
  376.6 70.4 %reduce-scatter.22.cloned.1.call-start = ((), (), s32[]{:S(2)}) async-start(), calls=%async_computation.24 | async-start | bytes 2359296 | tf_op jit(solution)/shard_map/reduce_scatter | solution.py:66
  437.5 22.1 %all-gather.28.cloned.1.call-start = ((), (), s32[]{:S(2)}) async-start(), calls=%async_computation.25 | async-start | bytes 2359296 | tf_op jit(solution)/shard_map/all_gather | solution.py:69
  447.0 98.4 %reduce-scatter.32.cloned.1.call-start = ((), (), s32[]{:S(2)}) async-start(), calls=%async_computation.31 | async-start | bytes 2359296 | tf_op jit(solution)/shard_map/reduce_scatter | solution.py:66
  530.2 25.6 %reduce-scatter.20.cloned.1.call-start = ((), (), s32[]{:S(2)}) async-start(), calls=%async_computation.22 | async-start | bytes 2359296 | tf_op jit(solution)/shard_map/reduce_scatter | solution.py:66
  545.4 22.9 %all-gather.32.cloned.1.call-start = ((), (), s32[]{:S(2)}) async-start(), calls=%async_computation.32 | async-start | bytes 2359296 | tf_op jit(solution)/shard_map/all_gather | solution.py:69
  546.0 34.8 %all-gather.26.cloned.1.call-start = ((), (), s32[]{:S(2)}) async-start(), calls=%async_computation.23 | async-start | bytes 2359296 | tf_op jit(solution)/shard_map/all_gather | solution.py:69
  555.8 109.9 %reduce-scatter.30.cloned.1.call-start = ((), (), s32[]{:S(2)}) async-start(), calls=%async_computation.29 | async-start | bytes 2359296 | tf_op jit(solution)/shard_map/reduce_scatter | solution.py:66
  655.3 63.8 %all-gather.30.cloned.1.call-start = ((), (), s32[]{:S(2)}) async-start(), calls=%async_computation.30 | async-start | bytes 2359296 | tf_op jit(solution)/shard_map/all_gather | solution.py:69
  665.7 156.2 %reduce-scatter.28.cloned.1.call-start = ((), (), s32[]{:S(2)}) async-start(), calls=%async_computation.28 | async-start | bytes 5013504 | tf_op jit(solution)/shard_map/reduce_scatter | solution.py:382
  680.2 284.4 %reduce-scatter.26.cloned.1.call-start = ((), (), s32[]{:S(2)}) async-start(), calls=%async_computation.27 | async-start | bytes 5013504 | tf_op jit(solution)/shard_map/reduce_scatter | solution.py:381
  691.3 401.6 %reduce-scatter.24.cloned.1.call-start = ((), (), s32[]{:S(2)}) async-start(), calls=%async_computation.26 | async-start | bytes 1253376 | tf_op jit(solution)/shard_map/reduce_scatter | solution.py:380
  718.8 588.1 %all-reduce.5.cloned.1.call-start = ((), (), s32[]{:S(2)}) async-start(), calls=%async_computation.33 | async-start | bytes 11853824
  740.0 226.3 %copy-start.161 = (f32[768]{0:T(1024)S(1)}, f32[768]{0:T(1024)}, u32[]{:S(2)}) copy-start(f32[768]{0:T(1024)} %get-tuple-element.127) | copy-start | bytes 9220
  740.0 226.3 %copy-start.162 = (f32[768]{0:T(1024)S(1)}, f32[768]{0:T(1024)}, u32[]{:S(2)}) copy-start(f32[768]{0:T(1024)} %get-tuple-element.115) | copy-start | bytes 9220
  740.0 226.3 %copy-start.163 = (f32[768]{0:T(1024)S(1)}, f32[768]{0:T(1024)}, u32[]{:S(2)}) copy-start(f32[768]{0:T(1024)} %get-tuple-element.129) | copy-start | bytes 9220
  740.1 226.3 %copy-start.164 = (f32[768]{0:T(1024)S(1)}, f32[768]{0:T(1024)}, u32[]{:S(2)}) copy-start(f32[768]{0:T(1024)} %get-tuple-element.117) | copy-start | bytes 9220
  740.1 620.8 %copy-start.72 = (f32[128,768]{1,0:T(8,128)S(1)}, f32[128,768]{1,0:T(8,128)}, u32[]{:S(2)}) copy-start(f32[128,768]{1,0:T(8,128)} %param.39) | copy-start | bytes 1179652
  740.1 620.8 %copy-start.109 = (f32[128,768]{1,0:T(8,128)S(1)}, f32[128,768]{1,0:T(8,128)}, u32[]{:S(2)}) copy-start(f32[128,768]{1,0:T(8,128)} %param.49) | copy-start | bytes 1179652
  740.1 623.1 %copy-start.73 = (f32[768,128]{1,0:T(8,128)S(1)}, f32[768,128]{1,0:T(8,128)}, u32[]{:S(2)}) copy-start(f32[768,128]{1,0:T(8,128)} %param.40) | copy-start | bytes 1179652
  (202 other events, 2136.2 us)
Sparse Core Ops, SparseCore 0:
  11.3 64.5 all-gather.11
  129.6 4.9 reduce-scatter.11
  157.4 4.9 reduce-scatter.15
  163.8 10.9 all-gather.13
  178.1 63.4 all-gather.15
  244.8 61.0 all-gather.17
  307.5 8.6 all-gather.21
  318.4 10.2 reduce-scatter.13
  331.7 10.2 reduce-scatter.17
  343.3 10.9 all-gather.19
  376.7 5.6 all-gather.23
  437.6 9.3 reduce-scatter.21
  448.6 10.9 all-gather.27
  530.3 10.2 reduce-scatter.31
  545.5 10.2 reduce-scatter.19
  557.3 10.9 all-gather.31
  569.8 10.9 all-gather.25
  655.4 10.2 reduce-scatter.29
  667.2 10.9 all-gather.29
  683.3 138.5 reduce-scatter.27
  827.9 136.7 reduce-scatter.25
  969.4 123.3 reduce-scatter.23
  1100.4 206.3 all-reduce.4
where the time goes:
time: 1390 us; the launch traced here: 1380 us
  waiting for transfers between devices  674 us (48%)
  matrix products  238 us (17%)
  blocking collectives  209 us (15%)
  other arithmetic  167 us (12%)
  local copies, waits for them, and re-layouts  58.7 us (4%)
  between operations  28.3 us (2%)
    reduce_scatter x1, waiting for transfers between devices, per_device(): lax.psum_scatter(layer_total[2], 'dp', scatter_dimension=0, tiled=True)  141 us
    unnamed x24, waiting for transfers between devices  136 us
    reduce_scatter x1, waiting for transfers between devices, per_device(): lax.psum_scatter(layer_total[1], 'dp', scatter_dimension=1, tiled=True)  126 us
    reduce_scatter x1, waiting for transfers between devices, per_device(): lax.psum_scatter(layer_total[3], 'dp', scatter_dimension=1, tiled=True)  78.6 us
    psum x1, blocking collectives, per_device(): lax.psum((small_total[0], small_total[1], small_total[2], small_total[3],...  77.9 us
    all_gather x1, waiting for transfers between devices, per_device(): lax.all_gather(fc_local, 'dp', axis=0, tiled=True)  61.6 us
    all_gather x1, waiting for transfers between devices, per_device(): lax.all_gather(proj_local, 'dp', axis=1, tiled=True)  56.3 us
    all_gather x1, blocking collectives, per_device(): lax.all_gather(out_local, 'dp', axis=1, tiled=True)  49.9 us
  transfers between devices with their start and end apart: 23, of which 15 were waited for; matrix products, arithmetic and copies ran while one was open for 14% of the time, Pallas kernels for 0%

commit v1 on v0

v1 whole, which is shorter than its diff:
```python
import functools
import math

import jax
import jax.numpy as jnp
import numpy as np
from jax import lax
from jax.experimental import pallas as pl
from jax.experimental.pallas import tpu as pltpu
from jax.sharding import PartitionSpec as P

HEAD_DIM = 64
NB = 16
T_STEPS = 2000
STEP = 10

NORM_EPS = 1e-05
MASKED = -1e30
BETA_FIRST = 0.9
BETA_SECOND = 0.999
ADAM_EPS = 1e-08
MATRIX_RATE = 0.05
NORM_RATE = 0.5
WEIGHT_DECAY = 0.1
CLIP_NORM = 0.01

TILE = 256
SPAN = 128
WINDOW = 384
MESH = pl.DeviceIdType.MESH
F32 = jnp.float32
BF16 = jnp.bfloat16
VMEM_LIMIT = 62 * 2**20


def nn(left, right):
    return jnp.dot(left, right, preferred_element_type=F32)


def nt(left, right):
    return lax.dot_general(
        left, right, (((1,), (1,)), ((), ())), preferred_element_type=F32
    )


def sinusoid(where, width):
    half = width // 2
    freqs = jnp.exp(-math.log(10000.0) * jnp.arange(half, dtype=F32) / half)
    angles = where[:, None] * freqs[None, :]
    return jnp.concatenate([jnp.sin(angles), jnp.cos(angles)], axis=-1)


def place_table(length, width):
    half = width // 2
    freqs = np.exp(-math.log(10000.0) * np.arange(half, dtype=np.float64) / half)
    angles = np.arange(length, dtype=np.float64)[:, None] * freqs[None, :]
    return np.concatenate([np.sin(angles), np.cos(angles)], axis=-1).astype(np.float32)


def norm_stats(values):
    width = values.shape[-1]
    center = values - jnp.sum(values, axis=-1, keepdims=True) * (1.0 / width)
    spread = jnp.sum(center * center, axis=-1, keepdims=True) * (1.0 / width)
    rate = lax.rsqrt(spread + NORM_EPS)
    return center * rate, rate


def norm_back(unit, rate, gain, upstream):
    width = unit.shape[-1]
    scaled = upstream * gain
    first = jnp.sum(scaled, axis=-1, keepdims=True) * (1.0 / width)
    second = jnp.sum(scaled * unit, axis=-1, keepdims=True) * (1.0 / width)
    return rate * (scaled - first - unit * second)


def column_sum(values):
    return jnp.sum(values, axis=0, keepdims=True)


def rows_at(index, count):
    return pl.ds(pl.multiple_of(index * count, count), count)


def guarded(condition, action):
    if condition is None:
        action()
    else:
        pl.when(condition)(action)


def position():
    me = lax.axis_index("dp")
    return me, lax.axis_index("mp"), me // 4, lax.rem(me // 2, 2), lax.rem(me, 2)


def index_of(z, y, x):
    return z * 4 + y * 2 + x


def neighbours():
    me, core, z, y, x = position()
    up = (jnp.minimum(me + 4, 15), core)
    down = (jnp.maximum(me - 4, 0), core)
    across_x = (index_of(z, y, 1 - x), core)
    across_y = (index_of(z, 1 - y, x), core)
    return up, down, across_x, across_y, (me, 1 - core)


def remote(source, target, send_sem, recv_sem, device):
    return pltpu.make_async_remote_copy(
        src_ref=source,
        dst_ref=target,
        send_sem=send_sem,
        recv_sem=recv_sem,
        device_id=device,
        device_id_type=MESH,
    )


def meet(devices):
    me, core = position()[:2]
    barrier = pltpu.get_barrier_semaphore()
    for device in devices:

        @pl.when(jnp.logical_or(device[0] != me, device[1] != core))
        def greet():
            pl.semaphore_signal(barrier, inc=1, device_id=device, device_id_type=MESH)

    pl.semaphore_wait(barrier, len(devices) - 1)


class Exchange:
    def __init__(self, source, slots, send_sems, recv_sems, devices):
        self.source, self.slots = source, slots
        self.send_sems, self.recv_sems = send_sems, recv_sems
        me, core = position()[:2]
        self.devices = [
            (slot, device, jnp.logical_or(device[0] != me, device[1] != core))
            for slot, device in enumerate(devices)
        ]
        self.mine = me if len(devices) == 16 else 2 * me + core

    def copy(self, slot, device):
        return remote(
            self.source, self.slots.at[self.mine], self.send_sems.at[slot], self.recv_sems.at[self.mine], device
        )

    def start(self):
        for slot, device, other in self.devices:
            guarded(other, lambda: self.copy(slot, device).start())

    def arrive(self):
        for slot, device, other in self.devices:

            def wait():
                remote(
                    self.slots.at[slot], self.slots.at[slot], self.send_sems.at[slot], self.recv_sems.at[slot], device
                ).wait_recv()

            guarded(other, wait)

    def total(self):
        self.slots[self.mine] = self.source[...]
        value = self.slots[0]
        for slot in range(1, len(self.devices)):
            value = value + self.slots[slot]
        return value

    def finish(self):
        for slot, device, other in self.devices:
            guarded(other, lambda: self.copy(slot, device).wait_send())


def same_core():
    core = position()[1]
    return [(d, core) for d in range(16)]


def every_device():
    return [(d, c) for d in range(16) for c in range(2)]


class Gather:
    def __init__(self, shard, whole, sems, rows, swapped):
        self.shard, self.whole, self.rows, self.swapped = shard, whole, rows, swapped
        (self.local_s, self.up_s, self.down_s, self.x_s, self.y_s, self.pair_s, self.recv, self.pair_recv) = sems
        self.up, self.down, self.xn, self.yn, self.pair = neighbours()
        self.me, self.core, self.z, self.y, self.x = position()
        self.sends = []

    def piece(self, b, c, d):
        return self.whole.at[b, c, rows_at(d, self.rows), :]

    def send(self, b, d, own, device, sem, condition=None, to_pair=False):
        source = self.shard.at[b] if own else self.piece(b, self.core, d)
        recv = self.pair_recv if to_pair else self.recv

        def copy():
            return remote(source, self.piece(b, self.core, d), sem, recv.at[b, d], device)

        self.sends.append((condition, copy))
        guarded(condition, lambda: copy().start())

    def arrive(self, b, c, d, recv):
        remote(self.piece(b, c, d), self.piece(b, c, d), self.pair_s.at[b, d], recv.at[b, d], self.pair).wait_recv()

    def first_second(self, b):
        if self.swapped(b):
            return (self.yn, self.y_s), (self.xn, self.x_s)
        return (self.xn, self.x_s), (self.yn, self.y_s)

    def spread(self, b, d, zz, own=False, condition=None):
        (first, first_s), (second, second_s) = self.first_second(b)
        self.send(b, d, own, first, first_s.at[b, zz], condition)
        self.send(b, d, own, second, second_s.at[b, 4 + zz], condition)
        self.send(b, d, own, self.pair, self.pair_s.at[b, d], condition, True)

    def local(self, b):
        return pltpu.make_async_copy(self.shard.at[b], self.piece(b, self.core, self.me), self.local_s.at[b])

    def begin(self, b):
        self.local(b).start()
        self.send(b, self.me, True, self.up, self.up_s.at[b, 0], self.z < 3)
        self.send(b, self.me, True, self.down, self.down_s.at[b, 0], self.z > 0)
        self.spread(b, self.me, self.z, True)

    def hop(self, b, distance):
        z = self.z
        for sign in (1, -1):
            if sign == 1:
                source, there, onward = jnp.maximum(z - distance, 0), z >= distance, z < 3
                device, sem = self.up, self.up_s
            else:
                source, there, onward = jnp.minimum(z + distance, 3), z + distance <= 3, z > 0
                device, sem = self.down, self.down_s
            d = index_of(source, self.y, self.x)
            guarded(there, lambda: self.arrive(b, self.core, d, self.recv))
            if distance < 3:
                self.send(b, d, False, device, sem.at[b, distance], jnp.logical_and(there, onward))
            self.spread(b, d, source, False, there)

    def turn(self, b):
        second, second_s = self.first_second(b)[1]
        yy, xx = (1 - self.y, self.x) if self.swapped(b) else (self.y, 1 - self.x)
        for zz in range(4):
            d = index_of(zz, yy, xx)
            self.arrive(b, self.core, d, self.recv)
            self.send(b, d, False, second, second_s.at[b, zz])
            self.send(b, d, False, self.pair, self.pair_s.at[b, d], None, True)

    def last(self, b):
        yy, xx = (self.y, 1 - self.x) if self.swapped(b) else (1 - self.y, self.x)
        for zz in range(4):
            for d in (index_of(zz, yy, xx), index_of(zz, 1 - self.y, 1 - self.x)):
                self.arrive(b, self.core, d, self.recv)
                self.send(b, d, False, self.pair, self.pair_s.at[b, d], None, True)

    def ready(self, b):
        self.local(b).wait()
        for d in range(16):
            self.arrive(b, 1 - self.core, d, self.pair_recv)

    def finish(self):
        for condition, copy in self.sends:
            guarded(condition, lambda copy=copy: copy().wait_send())


def gather_sems(count):
    dma = pltpu.SemaphoreType.DMA
    return [dma((count,)), dma((count, 4)), dma((count, 4)), dma((count, 8)), dma((count, 8)), dma((count, 16)), dma((count, 16)), dma((count, 16))]


class Scatter:
    def __init__(self, own, landed, loaded, near, far, base, stage, risen, fallen, out, sems, rows, swapped):
        self.own, self.landed, self.loaded, self.near, self.far = own, landed, loaded, near, far
        self.base, self.stage, self.risen, self.fallen, self.out = base, stage, risen, fallen, out
        (self.pair_s, self.pair_r, self.load_s, self.near_s, self.near_r, self.far_s, self.far_r, self.line_s, self.risen_r, self.fallen_r) = sems
        self.rows, self.swapped = rows, swapped
        self.up, self.down, self.xn, self.yn, self.pair = neighbours()
        self.me, self.core, self.z, self.y, self.x = position()

    def piece(self, b, zz, yy, xx):
        return self.own.at[b, rows_at(index_of(zz, yy, xx), self.rows), :]

    def pair_copy(self, b, source):
        return remote(source, self.landed.at[b], self.pair_s.at[b], self.pair_r.at[b], self.pair)

    def near_copy(self, b, zz, i):
        if self.swapped(b):
            place, device = (zz, i, 1 - self.x), self.xn
        else:
            place, device = (zz, 1 - self.y, i), self.yn
        return remote(
            self.piece(b, *place), self.near.at[b, zz, i], self.near_s.at[b, zz, i], self.near_r.at[b, zz, i], device
        )

    def far_place(self, b, zz):
        return (zz, 1 - self.y, self.x) if self.swapped(b) else (zz, self.y, 1 - self.x)

    def far_copy(self, b, zz):
        return remote(
            self.piece(b, *self.far_place(b, zz)), self.far.at[b, zz], self.far_s.at[b, zz], self.far_r.at[b, zz],
            self.yn if self.swapped(b) else self.xn,
        )

    def rise(self, b, t):
        return remote(self.stage.at[b, t], self.risen.at[b, t], self.line_s.at[b, t], self.risen_r.at[b, t], self.up)

    def fall(self, b, t):
        return remote(self.stage.at[b, t], self.fallen.at[b, t], self.line_s.at[b, t], self.fallen_r.at[b, t], self.down)

    def first(self, b):
        self.pair_copy(b, self.own.at[b]).wait_recv()
        load = pltpu.make_async_copy(self.landed.at[b], self.loaded, self.load_s.at[0])
        load.start()
        load.wait()

        def add(d, carry):
            at = rows_at(d, self.rows)
            self.own[b, at, :] = (self.own[b, at, :].astype(F32) + self.loaded[at, :].astype(F32)).astype(self.own.dtype)
            return carry

        lax.fori_loop(0, 16, add, 0)
        for zz in range(4):
            for i in range(2):
                self.near_copy(b, zz, i).start()

    def second(self, b):
        i = 1 - self.y if self.swapped(b) else 1 - self.x
        for zz in range(4):
            for j in range(2):
                self.near_copy(b, zz, j).wait_recv()
            place = self.far_place(b, zz)
            value = self.piece(b, *place)[...].astype(F32) + self.near[b, zz, i].astype(F32)
            self.piece(b, *place)[...] = value.astype(self.own.dtype)
            self.far_copy(b, zz).start()

    def line(self, b):
        z = self.z
        i = self.y if self.swapped(b) else self.x
        for zz in range(4):
            self.far_copy(b, zz).wait_recv()
            piece = self.piece(b, zz, self.y, self.x)[...].astype(F32)
            self.base[zz] = piece + self.near[b, zz, i].astype(F32) + self.far[b, zz].astype(F32)
        for t in (3, 2, 1):

            @pl.when(z < t)
            def going_up():
                @pl.when(z > 0)
                def add():
                    self.rise(b, t).wait_recv()
                    self.base[t] += self.risen[b, t].astype(F32)

                self.stage[b, t] = self.base[t].astype(self.stage.dtype)
                self.rise(b, t).start()

        for t in (0, 1, 2):

            @pl.when(z > t)
            def going_down():
                @pl.when(z < 3)
                def add():
                    self.fall(b, t).wait_recv()
                    self.base[t] += self.fallen[b, t].astype(F32)

                self.stage[b, t] = self.base[t].astype(self.stage.dtype)
                self.fall(b, t).start()

        self.out[b] = self.base[z]

    def result(self, b):
        z = self.z

        @pl.when(z > 0)
        def from_below():
            self.rise(b, z).wait_recv()
            self.out[b] += self.risen[b, z].astype(F32)

        @pl.when(z < 3)
        def from_above():
            self.fall(b, z).wait_recv()
            self.out[b] += self.fallen[b, z].astype(F32)

        value = self.out[b]
        return jnp.sum(value * value, keepdims=True)

    def finish(self, b):
        for zz in range(4):
            for i in range(2):
                self.near_copy(b, zz, i).wait_send()
            self.far_copy(b, zz).wait_send()
            guarded(self.z != zz, lambda: self.rise(b, zz).wait_send())


SCATTER_REFS = 18


def scatter_scratch(count, rows, columns):
    dma, vmem = pltpu.SemaphoreType.DMA, pltpu.VMEM
    return [
        vmem((count, 16 * rows, columns), BF16),
        vmem((16 * rows, columns), BF16),
        vmem((count, 4, 2, rows, columns), BF16),
        vmem((count, 4, rows, columns), BF16),
        vmem((4, rows, columns), F32),
        vmem((count, 4, rows, columns), BF16),
        vmem((count, 4, rows, columns), BF16),
        vmem((count, 4, rows, columns), BF16),
        dma((count,)), dma((count,)), dma((1,)), dma((count, 4, 2)), dma((count, 4, 2)),
        dma((count, 4)), dma((count, 4)), dma((count, 4)), dma((count, 4)), dma((count, 4)),
    ]


def scatter_of(refs, landed, out, rows, swapped):
    own, loaded, near, far, base, stage, risen, fallen = refs[:8]
    return Scatter(own, landed, loaded, near, far, base, stage, risen, fallen, out, refs[8:], rows, swapped)


def gelu_parts(values):
    root = 0.7978845608028654
    square = values * values
    bent = jnp.tanh(root * (values + 0.044715 * (square * values)))
    half = 0.5 * (1.0 + bent)
    slope = half + (0.5 * root) * values * (1.0 - bent * bent) * (1.0 + (3 * 0.044715) * square)
    return values * half, slope


def halves_of(shape, axis, scale):
    low = lax.broadcasted_iota(jnp.int32, shape, axis) < HEAD_DIM
    return jnp.where(low, scale, 0.0).astype(BF16), jnp.where(low, 0.0, scale).astype(BF16)


def pick_halves(wide):
    low = lax.broadcasted_iota(jnp.int32, (2 * HEAD_DIM, SPAN), 0) < HEAD_DIM
    return jnp.where(low, wide[:, :SPAN], wide[:, SPAN:])


def window_start(block, blocks):
    return min(max(block - 1, 0), blocks - WINDOW // SPAN) * SPAN


def forward_kernel(fused, shapes, *refs):
    length, width, pairs = shapes
    blocks = length // SPAN
    tiles = length // TILE
    (
        shard, count_in, tok, seg_col, seg_row, noise, embed3, up_low, norms, places, time_row, mix,
        whole, count_out, start, noisy, zero_out, one_out, two_out, qkv_out, keyt_out, att_out, probs_out, act_out, slope_out, first_t_out, second_t_out,
        h_zero, h_one, h_two, normed, normed_t, qkv, key_t, value_t, att, probs, act, slope, weights, bias,
        out_sems, probs_sems, weight_sems,
    ) = refs[:44]
    core = lax.axis_index("mp")
    saves = []

    def save(source, target):
        copy = pltpu.make_async_copy(source, target, out_sems.at[len(saves)])
        copy.start()
        saves.append(copy)

    if fused:
        rest = refs[44:]
        gather = Gather(shard, whole, rest[:8], shard.shape[1], lambda b: b % 2 == 1)
        counts, count_send, count_recv = rest[8:]
        meet(same_core() + [neighbours()[4]])
        exchange = Exchange(count_in, counts, count_send, count_recv, same_core())
        exchange.start()
        for b in range(6):
            gather.begin(b)
    else:
        gather = None

    def pump(*steps):
        if gather is not None:
            for name, b, *more in steps:
                getattr(gather, name)(b, *more)

    def load(b, c, slot):
        return pltpu.make_async_copy((whole if fused else shard).at[b, c], weights.at[slot], weight_sems.at[slot])

    def embed_tile(r):
        at = rows_at(r, TILE)
        hot = (tok[at, :] == lax.broadcasted_iota(jnp.int32, (TILE, embed3.shape[0]), 1)).astype(F32).astype(BF16)
        thirds = nn(hot, embed3[...])
        e = thirds.shape[1] // 3
        first = thirds[:, :e] + thirds[:, e : 2 * e] + thirds[:, 2 * e :]
        start[at, :] = first
        low = (mix[0, 0] * first + mix[0, 1] * noise[at, :]).astype(BF16)
        noisy[at, :] = low
        hidden = nn(low, up_low[...]) + places[at, :] + time_row[...]
        h_zero[at, :] = hidden
        unit = norm_stats(hidden)[0]
        scaled = unit * norms[0:1, :] + norms[1:2, :]
        normed[at, :] = scaled.astype(BF16)
        normed_t[0, :, at] = scaled.T.astype(BF16)

    steps = [
        [("hop", 0, 1), ("hop", 1, 1), ("hop", 2, 1), ("hop", 3, 1)],
        [("hop", 4, 1), ("hop", 5, 1), ("hop", 0, 2), ("hop", 1, 2)],
        [("hop", 2, 2), ("hop", 3, 2), ("hop", 0, 3), ("hop", 1, 3)],
        [("hop", 4, 2), ("hop", 5, 2), ("turn", 0), ("turn", 1)],
    ]
    for r in range(tiles):
        embed_tile(r)
        if r < 4:
            pump(*steps[r])
    save(h_zero, zero_out)
    save(normed_t.at[0], first_t_out)
    for i in range(blocks):
        w0 = window_start(i, blocks)
        same = seg_col[w0 : w0 + WINDOW, :] == seg_row[:, i * SPAN : (i + 1) * SPAN]
        bias[i] = jnp.where(same, 0.0, MASKED)
    pump(("hop", 2, 3), ("hop", 3, 3), ("hop", 4, 3), ("hop", 5, 3), ("last", 0), ("last", 1), ("turn", 2), ("turn", 3))
    pump(("ready", 0), ("ready", 1))
    for b in range(2):
        for c in range(2):
            load(b, c, 2 * b + c).start()
    for b in range(2):
        for c in range(2):
            load(b, c, 2 * b + c).wait()
    half = width // 2
    for c in range(2):

        def project(r, carry):
            at = rows_at(r, TILE)
            rows = normed[at, :]
            first = nn(rows, weights[c])
            values = nn(rows, weights[2 + c, :, :half])
            cols = slice(c * half, (c + 1) * half)
            qkv[0, at, cols] = first[:, :half].astype(BF16)
            qkv[1, at, cols] = first[:, half:].astype(BF16)
            qkv[2, at, cols] = values.astype(BF16)
            key_t[cols, at] = first[:, half:].T.astype(BF16)
            value_t[cols, at] = values.T.astype(BF16)
            return carry

        lax.fori_loop(0, tiles, project, 0)
    for j in range(3):
        save(qkv.at[j], qkv_out.at[j])
    save(key_t, keyt_out)

    def probs_copy(pair, slot):
        return pltpu.make_async_copy(probs.at[slot], probs_out.at[pl.ds(pair * blocks, blocks)], probs_sems.at[slot])

    low, high = halves_of((1, SPAN), 1, 0.125)

    def attend(pair, carry):
        slot = lax.rem(pair, 2)
        cols = pl.ds(pl.multiple_of(pair * SPAN, SPAN), SPAN)

        @pl.when(pair >= 2)
        def free():
            probs_copy(pair - 2, slot).wait()

        for i in range(blocks):
            w0 = window_start(i, blocks)
            queries = qkv[0, i * SPAN : (i + 1) * SPAN, cols]
            both = jnp.concatenate([queries * low, queries * high], axis=0)
            scores = nt(qkv[1, w0 : w0 + WINDOW, cols], both)
            mask = bias[i]
            scores = scores + jnp.concatenate([mask, mask], axis=1)
            most = jnp.max(scores, axis=0, keepdims=True)
            raised = jnp.exp(scores - most)
            share = 1.0 / jnp.sum(raised, axis=0, keepdims=True)
            prob = (raised * share).astype(BF16)
            probs[slot, i] = prob
            mixed = nn(value_t[cols, w0 : w0 + WINDOW], prob)
            att[i * SPAN : (i + 1) * SPAN, cols] = pick_halves(mixed).T.astype(BF16)
        probs_copy(pair, slot).start()
        return carry

    middle = [[("turn", 4), ("turn", 5)], [("last", 2), ("last", 3)], []]
    for step in range(3):
        lax.fori_loop(step * pairs // 3, (step + 1) * pairs // 3, attend, 0)
        pump(*middle[step])
    for pair in (pairs - 2, pairs - 1):
        probs_copy(pair, pair % 2).wait()
    save(att, att_out)

    def after_attention(r, carry):
        at = rows_at(r, TILE)
        mixed = att[at, :]
        total = nt(mixed[:, :half], weights[2, :, half:]) + nt(mixed[:, half:], weights[3, :, half:])
        hidden = h_zero[at, :] + total
        h_one[at, :] = hidden
        unit = norm_stats(hidden)[0]
        scaled = unit * norms[2:3, :] + norms[3:4, :]
        normed[at, :] = scaled.astype(BF16)
        normed_t[1, :, at] = scaled.T.astype(BF16)
        return carry

    lax.fori_loop(0, tiles, after_attention, 0)
    save(h_one, one_out)
    save(normed_t.at[1], second_t_out)
    pump(("ready", 2), ("ready", 3))
    for h in range(2):
        for c in range(2):
            load(2 + h, c, 4 + 2 * h + c).start()
    for j in range(4):
        load(2 + j // 2, j % 2, 4 + j).wait()

        def grow(r, carry):
            at = rows_at(r, TILE)
            before = nn(normed[at, :], weights[4 + j])
            active, bend = gelu_parts(before)
            act[j, at, :] = active.astype(BF16)
            slope[j, at, :] = bend.astype(BF16)
            return carry

        lax.fori_loop(0, tiles, grow, 0)
        save(act.at[j], act_out.at[j])
        save(slope.at[j], slope_out.at[j])
        if j == 1:
            pump(("last", 4), ("last", 5))
    pump(("ready", 4), ("ready", 5))
    for h in range(2):
        for c in range(2):
            load(4 + h, c, 2 * h + c).start()
    for j in range(4):
        load(4 + j // 2, j % 2, j).wait()

    def shrink(r, carry):
        at = rows_at(r, TILE)
        total = h_one[at, :]
        for j in range(4):
            total = total + nt(act[j, at, :], weights[j])
        h_two[at, :] = total
        return carry

    lax.fori_loop(0, tiles, shrink, 0)
    save(h_two, two_out)
    if fused:
        exchange.arrive()
        count_out[...] = exchange.total()
        gather.finish()
        exchange.finish()
    else:
        count_out[...] = count_in[...]
    for copy in saves:
        copy.wait()


def run_forward(fused, source, count_in, tok, seg_col, seg_row, noise, embed3, up_low, norms, places, time_row, mix):
    length, width = places.shape
    pairs = width // SPAN
    blocks = length // SPAN
    dma, vmem = pltpu.SemaphoreType.DMA, pltpu.VMEM
    anywhere, inside = pl.BlockSpec(memory_space=pl.ANY), pl.BlockSpec(memory_space=pltpu.VMEM)
    emb = noise.shape[1]

    def made(shape, dtype=BF16):
        return jax.ShapeDtypeStruct(shape, dtype)

    out_shape = [
        made((6, 2, width, width)),
        made(count_in.shape, F32),
        made((length, emb), F32),
        made((length, emb)),
        made((length, width), F32),
        made((length, width), F32),
        made((length, width), F32),
        made((3, length, width)),
        made((width, length)),
        made((length, width)),
        made((pairs * blocks, WINDOW, 2 * SPAN)),
        made((4, length, width)),
        made((4, length, width)),
        made((width, length)),
        made((width, length)),
    ]
    scratch = [
        vmem((length, width), F32),
        vmem((length, width), F32),
        vmem((length, width), F32),
        vmem((length, width), BF16),
        vmem((2, width, length), BF16),
        vmem((3, length, width), BF16),
        vmem((width, length), BF16),
        vmem((width, length), BF16),
        vmem((length, width), BF16),
        vmem((2, blocks, WINDOW, 2 * SPAN), BF16),
        vmem((4, length, width), BF16),
        vmem((4, length, width), BF16),
        vmem((8, width, width), BF16),
        vmem((blocks, WINDOW, SPAN), F32),
        dma((20,)),
        dma((2,)),
        dma((8,)),
    ]
    if fused:
        scratch += gather_sems(6) + [vmem((16,) + count_in.shape, F32), dma((16,)), dma((16,))]
        params = pltpu.CompilerParams(collective_id=0, has_side_effects=True, vmem_limit_bytes=VMEM_LIMIT)
    else:
        params = pltpu.CompilerParams(vmem_limit_bytes=VMEM_LIMIT)
    results = pl.pallas_call(
        functools.partial(forward_kernel, fused, (length, width, pairs)),
        out_shape=out_shape,
        in_specs=[anywhere] + [inside] * 10 + [pl.BlockSpec(memory_space=pltpu.SMEM)],
        out_specs=[anywhere, inside, inside, inside] + [anywhere] * 11,
        scratch_shapes=scratch,
        compiler_params=params,
        name="forward",
    )(source, count_in, tok, seg_col, seg_row, noise, embed3, up_low, norms, places, time_row, mix)
    return results


def backward_kernel(fused, shapes, *refs):
    length, width, pairs = shapes
    blocks = length // SPAN
    tiles = length // TILE
    half = width // 2
    (
        whole, columns, start, noisy, zero_in, one_in, two_in, qkv_in, keyt_in, att_in, probs_in, act_in, slope_in, first_t_in, second_t_in,
        embed_low, pad_row, up_low, down_low, norms, mix,
        out_blocks, out_small, out_loss, landed, small_landed,
        hidden, grad, back, branch, branch_t, normed_t, pre, slots, weights, acc, probs, error, small, norm_grads, posted, small_own, scalars,
        load_sems, slot_sems, weight_sems, probs_sems, post_sems,
    ) = refs[:48]
    core = lax.axis_index("mp")
    emb = start.shape[1]
    vocab = embed_low.shape[0]
    side = width // TILE

    if fused:
        rest = refs[48:]
        main_refs, rest = rest[:SCATTER_REFS], rest[SCATTER_REFS:]
        tiny_refs, rest = rest[:SCATTER_REFS], rest[SCATTER_REFS:]
        tiny_shard, tiny_whole, tiny_out, slots_all, all_send, all_recv = rest[:6]
        gather_refs = rest[6:]
        main = scatter_of(main_refs, landed, out_blocks, width // 16, lambda b: b in (1, 4, 5))
        tiny = scatter_of(tiny_refs, small_landed, tiny_out, 16, lambda b: False)
        own, tiny_own = main.own, tiny.own
        devices = every_device()
        meet(devices)
    else:
        own = small_own = None

    def pump(*steps):
        if fused:
            for name, b in steps:
                getattr(main, name)(b)

    def post(b, slot):
        if fused:
            main.pair_copy(b, posted.at[slot]).start()
        else:
            pltpu.make_async_copy(posted.at[slot], out_blocks.at[b, 1 - core], post_sems.at[slot]).start()

    def posted_wait(b, slot):
        if fused:
            main.pair_copy(b, posted.at[slot]).wait_send()
        else:
            pltpu.make_async_copy(posted.at[slot], out_blocks.at[b, 1 - core], post_sems.at[slot]).wait()

    def fetch(source, target, k):
        copy = pltpu.make_async_copy(source, target, load_sems.at[k])
        copy.start()
        return copy

    def load_weights(b, c, slot):
        return pltpu.make_async_copy(whole.at[b, c], weights.at[slot], weight_sems.at[slot])

    def load_slot(source, slot):
        return pltpu.make_async_copy(source, slots.at[slot], slot_sems.at[slot])

    def feed(s):
        h, c = s // 2, (1 - core if s % 2 == 0 else core)
        first = 2 * (s % 2)
        return [
            load_weights(2 + h, c, first),
            load_weights(4 + h, c, first + 1),
            load_slot(act_in.at[2 * h + c], first),
            load_slot(slope_in.at[2 * h + c], first + 1),
        ]

    two_copy = fetch(two_in, hidden, 0)
    normed_copy = fetch(second_t_in, normed_t, 1)
    for copy in feed(0):
        copy.start()
    norm_grads[...] = jnp.zeros(norm_grads.shape, F32)
    small[...] = jnp.zeros(small.shape, F32)
    two_copy.wait()
    ids = lax.broadcasted_iota(jnp.int32, (TILE, vocab), 1).astype(F32)
    d0, u0, e0 = 0, width, 2 * width

    def add_norm(row, upstream, unit):
        norm_grads[row : row + 1, :] += column_sum(upstream * unit)
        norm_grads[row + 1 : row + 2, :] += column_sum(upstream)

    def head(r, loss):
        at = rows_at(r, TILE)
        unit, rate = norm_stats(hidden[at, :])
        ended = (unit * norms[4:5, :] + norms[5:6, :]).astype(BF16)
        predicted = nn(ended, down_low[...])
        pred_low = predicted.astype(BF16)
        logits = nt(pred_low, embed_low[...]) + pad_row[...]
        most = jnp.max(logits, axis=-1, keepdims=True)
        raised = jnp.exp(logits - most)
        total = jnp.sum(raised, axis=-1, keepdims=True)
        hit = columns[at, 0:1] == ids
        picked = jnp.sum(jnp.where(hit, logits, 0.0), axis=-1, keepdims=True)
        miss = predicted - start[at, :]
        per_token = jnp.sum(miss * miss, axis=-1, keepdims=True) * (1.0 / emb) + (jnp.log(total) + most) - picked
        loss = loss + jnp.sum(columns[at, 1:2] * per_token, keepdims=True)
        coef = columns[at, 2:3]
        grad_logits = (coef * (raised * (1.0 / total) - jnp.where(hit, 1.0, 0.0))).astype(BF16)
        grad_error = coef * 2.0 * miss * (1.0 / emb)
        error[at, :] = grad_error
        grad_pred = nn(grad_logits, embed_low[...]) + grad_error
        grad_pred_low = grad_pred.astype(BF16)
        small[:, d0 : d0 + width] += nn(grad_pred.T.astype(BF16), ended)
        small[:, e0 : e0 + vocab] += nn(predicted.T.astype(BF16), grad_logits)
        upstream = nt(grad_pred_low, down_low[...])
        add_norm(4, upstream, unit)
        result = norm_back(unit, rate, norms[4:5, :], upstream)
        grad[at, :] = result
        branch[at, :] = result.astype(BF16)
        branch_t[:, at] = result.T.astype(BF16)
        return loss

    loss = lax.fori_loop(0, tiles, head, jnp.zeros((1, 1), F32))
    one_copy = fetch(one_in, hidden, 0)
    normed_copy.wait()

    for s in range(4):
        h = s // 2
        if s < 3:
            for copy in feed(s + 1):
                copy.start()
        for copy in feed(s):
            copy.wait()
        first = 2 * (s % 2)
        fc, proj, active, bend = weights.at[first], weights.at[first + 1], slots.at[first], slots.at[first + 1]

        def slide(r, carry):
            at = rows_at(r, TILE)
            through = nn(branch[at, :], proj[...])
            pushed = (through * bend[at, :].astype(F32)).astype(BF16)
            pre[at, :] = pushed
            value = nt(pushed, fc[...])
            if s == 0:
                back[at, :] = value
            else:
                back[at, :] += value
            return carry

        lax.fori_loop(0, tiles, slide, 0)
        mine = s % 2 == 1
        if s == 2:
            posted_wait(2, 0)
            posted_wait(4, 1)

        def weigh(m, carry):
            at = rows_at(m, TILE)
            fc_grad = nn(normed_t[at, :], pre[...]).astype(BF16)
            proj_grad = nn(branch_t[at, :], active[...]).astype(BF16)
            if mine and fused:
                own[2 + h, at, :] = fc_grad
                own[4 + h, at, :] = proj_grad
            else:
                posted[2 if mine else 0, at, :] = fc_grad
                posted[3 if mine else 1, at, :] = proj_grad
            return carry

        if mine and not fused and s == 3:
            for slot, b in ((2, 2), (3, 4)):
                pltpu.make_async_copy(posted.at[slot], out_blocks.at[b, core], post_sems.at[slot]).wait()
        lax.fori_loop(0, side, weigh, 0)
        if not mine:
            post(2 + h, 0)
            post(4 + h, 1)
        elif not fused:
            for slot, b in ((2, 2 + h), (3, 4 + h)):
                pltpu.make_async_copy(posted.at[slot], out_blocks.at[b, core], post_sems.at[slot]).start()
        if s == 1:
            pump(("first", 2), ("first", 4))
        if s == 2:
            pump(("second", 2), ("second", 4))
        if s == 3:
            pump(("first", 3), ("first", 5))

    for c in range(2):
        load_weights(0, c, c).start()
        load_weights(1, c, 2 + c).start()
    att_copy = fetch(att_in, pre, 2)
    first_t_copy = fetch(first_t_in, normed_t, 1)
    load_slot(qkv_in.at[0], 0).start()
    load_slot(qkv_in.at[2], 2).start()
    one_copy.wait()

    def through_two(r, carry):
        at = rows_at(r, TILE)
        unit, rate = norm_stats(hidden[at, :])
        upstream = back[at, :]
        add_norm(2, upstream, unit)
        result = grad[at, :] + norm_back(unit, rate, norms[2:3, :], upstream)
        grad[at, :] = result
        branch[at, :] = result.astype(BF16)
        branch_t[:, at] = result.T.astype(BF16)
        return carry

    lax.fori_loop(0, tiles, through_two, 0)
    zero_copy = fetch(zero_in, hidden, 0)
    pump(("second", 3), ("second", 5), ("line", 2), ("line", 4))
    att_copy.wait()
    posted_wait(3, 0)
    posted_wait(5, 1)
    if not fused:
        for slot, b in ((2, 3), (3, 5)):
            pltpu.make_async_copy(posted.at[slot], out_blocks.at[b, core], post_sems.at[slot]).wait()

    def other_half(c):
        return pl.ds(pl.multiple_of(c * half, SPAN), half)

    def store(which, b, at, cols, value):
        if which == 1 and fused:
            own[b, at, cols] = value
        else:
            posted[2 * which + (1 - b), at, cols] = value

    def out_weigh(m, carry):
        at = rows_at(m, TILE)
        for which in range(2):
            c = core if which else 1 - core
            store(which, 1, at, slice(half, width), nn(branch_t[at, :], pre[:, other_half(c)]).astype(BF16))
        return carry

    lax.fori_loop(0, side, out_weigh, 0)
    for c in range(2):
        load_weights(0, c, c).wait()
        load_weights(1, c, 2 + c).wait()
    keyt_copy = fetch(keyt_in, branch_t, 3)

    def spread_att(r, carry):
        at = rows_at(r, TILE)
        rows = branch[at, :]
        for c in range(2):
            slots[3, at, c * half : (c + 1) * half] = nn(rows, weights[2 + c, :, half:]).astype(BF16)
        return carry

    lax.fori_loop(0, tiles, spread_att, 0)
    count = blocks // 2

    def probs_copy(unit):
        slot = lax.rem(unit, 2)
        return pltpu.make_async_copy(probs_in.at[pl.ds(unit * count, count)], probs.at[slot], probs_sems.at[slot])

    probs_copy(0).start()
    load_slot(qkv_in.at[0], 0).wait()
    load_slot(qkv_in.at[2], 2).wait()
    keyt_copy.wait()
    low, high = halves_of((1, SPAN), 1, 0.125)
    low_one, high_one = halves_of((1, SPAN), 1, 1.0)

    def attend(pair, carry):
        cols = pl.ds(pl.multiple_of(pair * SPAN, SPAN), SPAN)
        acc[...] = jnp.zeros(acc.shape, F32)
        for part in range(2):
            unit = 2 * pair + part

            @pl.when(unit + 1 < 2 * pairs)
            def ahead():
                probs_copy(unit + 1).start()

            probs_copy(unit).wait()
            for k in range(count):
                i = part * count + k
                w0 = window_start(i, blocks)
                here = slice(i * SPAN, (i + 1) * SPAN)
                there = slice(w0, w0 + WINDOW)
                up_rows = slots[3, here, cols]
                ups = jnp.concatenate([up_rows * low_one, up_rows * high_one], axis=0)
                queries = slots[0, here, cols]
                asks = jnp.concatenate([queries * low, queries * high], axis=0)
                prob = probs[part, k]
                wide = prob.astype(F32)
                grad_probs = nt(slots[2, there, cols], ups)
                inner = jnp.sum(grad_probs * wide, axis=0, keepdims=True)
                grad_scores = (wide * (grad_probs - inner)).astype(BF16)
                acc[0, there, :] += nn(grad_scores, asks)
                acc[1, there, :] += nn(prob, ups)
                asked = nn(branch_t[cols, there], grad_scores)
                slots[0, here, cols] = (pick_halves(asked).T * 0.125).astype(BF16)
        slots[1, :, cols] = acc[0].astype(BF16)
        slots[2, :, cols] = acc[1].astype(BF16)
        return carry

    middle = [[("line", 3), ("line", 5)], [], []]
    for step in range(3):
        lax.fori_loop(step * pairs // 3, (step + 1) * pairs // 3, attend, 0)
        pump(*middle[step])
    first_t_copy.wait()

    def qkv_weigh(which):
        c = core if which else 1 - core
        cols = other_half(c)

        def body(m, carry):
            at = rows_at(m, TILE)
            rows = normed_t[at, :]
            store(which, 1, at, slice(0, half), nn(rows, slots[2, :, cols]).astype(BF16))
            store(which, 0, at, slice(0, half), nn(rows, slots[0, :, cols]).astype(BF16))
            store(which, 0, at, slice(half, width), nn(rows, slots[1, :, cols]).astype(BF16))
            return carry

        lax.fori_loop(0, side, body, 0)

    qkv_weigh(0)
    post(1, 0)
    post(0, 1)
    qkv_weigh(1)
    if not fused:
        for slot, b in ((2, 1), (3, 0)):
            pltpu.make_async_copy(posted.at[slot], out_blocks.at[b, core], post_sems.at[slot]).start()
    zero_copy.wait()
    pump(("first", 1), ("first", 0))

    def through_one(r, carry):
        at = rows_at(r, TILE)
        upstream = jnp.zeros((TILE, width), F32)
        for c in range(2):
            cols = slice(c * half, (c + 1) * half)
            upstream = upstream + nt(slots[0, at, cols], weights[c, :, :half])
            upstream = upstream + nt(slots[1, at, cols], weights[c, :, half:])
            upstream = upstream + nt(slots[2, at, cols], weights[2 + c, :, :half])
        unit, rate = norm_stats(hidden[at, :])
        add_norm(0, upstream, unit)
        grad_zero = (grad[at, :] + norm_back(unit, rate, norms[0:1, :], upstream)).astype(BF16)
        small[:, u0 : u0 + width] += nn(noisy[at, :].astype(F32).T.astype(BF16), grad_zero)
        grad_start = (mix[0, 0] * nt(grad_zero, up_low[...]) - error[at, :]).T
        upper = grad_start.astype(BF16)
        lower = (grad_start - upper.astype(F32)).astype(BF16)
        hot = (columns[at, 0:1] == ids).astype(F32).astype(BF16)
        small[:, e0 : e0 + vocab] += nn(upper, hot) + nn(lower, hot)
        return carry

    lax.fori_loop(0, tiles, through_one, 0)
    lanes = emb
    n0 = e0 + vocab
    for k in range(6):
        for j in range(width // lanes):
            row = k * (width // lanes) + j
            small[row : row + 1, n0 : n0 + lanes] = norm_grads[k : k + 1, j * lanes : (j + 1) * lanes]
    if not fused:
        out_small[...] = small[...]
        out_loss[...] = jnp.broadcast_to(loss, out_loss.shape)
        posted_wait(1, 0)
        posted_wait(0, 1)
        for slot, b in ((2, 1), (3, 0)):
            pltpu.make_async_copy(posted.at[slot], out_blocks.at[b, core], post_sems.at[slot]).wait()
        return

    group = small.shape[1] // 4
    for q in range(4):
        value = small[:, q * group : (q + 1) * group].astype(BF16)
        rows = slice((q % 2) * small.shape[0], (q % 2 + 1) * small.shape[0])
        mine = core == q // 2

        @pl.when(mine)
        def keep():
            tiny.own[0, rows, :] = value

        @pl.when(jnp.logical_not(mine))
        def give():
            small_own[rows, :] = value

    give_copy = tiny.pair_copy(0, small_own)
    give_copy.start()
    pump(("second", 1), ("second", 0))
    tiny.first(0)
    squares = main.result(2) + main.result(4)
    squares = squares + main.result(3) + main.result(5)
    tiny.second(0)
    pump(("line", 1), ("line", 0))
    tiny.line(0)
    squares = squares + tiny.result(0)
    squares = squares + main.result(1) + main.result(0)
    row = lax.broadcasted_iota(jnp.int32, scalars.shape, 0)
    scalars[...] = jnp.where(row == 0, squares, jnp.where(row == 1, loss, 0.0))
    exchange = Exchange(scalars, slots_all, all_send, all_recv, devices)
    exchange.start()
    tiny_shard[0] = tiny_out[0].astype(BF16)
    gather = Gather(tiny_shard, tiny_whole, gather_refs, 16, lambda b: False)
    gather.begin(0)
    for distance in (1, 2, 3):
        gather.hop(0, distance)
    gather.turn(0)
    gather.last(0)
    gather.ready(0)
    exchange.arrive()
    out_loss[...] = exchange.total()
    for q in range(4):
        rows = slice((q % 2) * small.shape[0], (q % 2 + 1) * small.shape[0])
        out_small[:, q * group : (q + 1) * group] = tiny_whole[0, q // 2, rows, :].astype(F32)
    posted_wait(1, 0)
    posted_wait(0, 1)
    give_copy.wait_send()
    gather.finish()
    exchange.finish()
    for b in range(6):
        main.finish(b)
    tiny.finish(0)


def run_backward(fused, whole, columns, start, noisy, kept, embed_low, pad_row, up_low, down_low, norms, mix):
    zero, one, two, qkv, key_t, att, probs, act, slope, first_t, second_t = kept
    length, width = zero.shape
    pairs = width // SPAN
    blocks = length // SPAN
    emb, vocab = start.shape[1], embed_low.shape[0]
    dma, vmem = pltpu.SemaphoreType.DMA, pltpu.VMEM
    anywhere, inside = pl.BlockSpec(memory_space=pl.ANY), pl.BlockSpec(memory_space=pltpu.VMEM)
    spread = 2 * width + vocab + emb
    group = spread // 4
    rows = width // 16

    def made(shape, dtype=BF16):
        return jax.ShapeDtypeStruct(shape, dtype)

    blocks_out = made((6, rows, width), F32) if fused else made((6, 2, width, width))
    out_shape = [blocks_out, made((emb, spread), F32), made((8, 128), F32)]
    out_shape += [made((6, width, width)) if fused else made((8, 128)), made((1, 2 * emb, group)) if fused else made((8, 128))]
    scratch = [
        vmem((length, width), F32),
        vmem((length, width), F32),
        vmem((length, width), F32),
        vmem((length, width), BF16),
        vmem((width, length), BF16),
        vmem((width, length), BF16),
        vmem((length, width), BF16),
        vmem((4, length, width), BF16),
        vmem((4, width, width), BF16),
        vmem((2, length, SPAN), F32),
        vmem((2, blocks // 2, WINDOW, 2 * SPAN), BF16),
        vmem((length, emb), F32),
        vmem((emb, spread), F32),
        vmem((8, width), F32),
        vmem((2 if fused else 4, width, width), BF16),
        vmem((2 * emb, group), BF16),
        vmem((8, 128), F32),
        dma((4,)),
        dma((4,)),
        dma((4,)),
        dma((2,)),
        dma((4,)),
    ]
    if fused:
        scratch += scatter_scratch(6, rows, width) + scatter_scratch(1, 16, group)
        scratch += [
            vmem((1, 16, group), BF16),
            vmem((1, 2, 2 * emb, group), BF16),
            vmem((1, 16, group), F32),
            vmem((32, 8, 128), F32),
            dma((32,)),
            dma((32,)),
        ] + gather_sems(1)
        params = pltpu.CompilerParams(collective_id=1, has_side_effects=True, vmem_limit_bytes=VMEM_LIMIT)
    else:
        params = pltpu.CompilerParams(vmem_limit_bytes=VMEM_LIMIT)
    return pl.pallas_call(
        functools.partial(backward_kernel, fused, (length, width, pairs)),
        out_shape=out_shape,
        in_specs=[anywhere] + [inside] * 3 + [anywhere] * 11 + [inside] * 5 + [pl.BlockSpec(memory_space=pltpu.SMEM)],
        out_specs=[inside if fused else anywhere, inside, inside, anywhere, anywhere],
        scratch_shapes=scratch,
        compiler_params=params,
        name="backward",
    )(whole, columns, start, noisy, zero, one, two, qkv, key_t, att, probs, act, slope, first_t, second_t, embed_low, pad_row, up_low, down_low, norms, mix)[:3]


def adam_update(weight, grad, first, second, rate, decay):
    first_new = BETA_FIRST * first + (1.0 - BETA_FIRST) * grad
    second_new = BETA_SECOND * second + (1.0 - BETA_SECOND) * grad * grad
    first_hat = first_new / (1.0 - BETA_FIRST**STEP)
    second_hat = second_new / (1.0 - BETA_SECOND**STEP)
    weight_new = weight - rate * (first_hat / (jnp.sqrt(second_hat) + ADAM_EPS) + decay * weight)
    return (first_new, second_new, weight_new)


def per_device(fused, token_ids, segment_ids, timesteps, noise, bucket_ids, counted, embed, up_weight, down_weight, qkv_weight, out_weight, fc_weight, proj_weight, norm_params, embed_m, embed_v, up_m, up_v, down_m, down_v, qkv_m, qkv_v, out_m, out_v, fc_m, fc_v, proj_m, proj_v, norm_m, norm_v):
    row = lax.axis_index("mp")
    length = token_ids.shape[1]
    vocab, emb = embed.shape
    width = up_weight.shape[1]
    half = width // 2
    hidden = fc_weight.shape[1] // 2

    def my(array):
        return lax.dynamic_index_in_dim(array, row, 0, keepdims=False)

    live = counted.astype(F32)
    hot = (bucket_ids[..., None] == jnp.arange(NB)[None, None, :]).astype(F32)
    local_counts = jnp.sum(live[..., None] * hot, axis=(0, 1))
    tokens, segments, step, row_noise = my(token_ids), my(segment_ids), my(timesteps), my(noise)
    keep = 1.0 - jnp.sqrt(step.astype(F32) / T_STEPS + 0.0001)
    mix = jnp.stack([jnp.sqrt(keep), jnp.sqrt(1.0 - keep)])[None]
    time_row = sinusoid(step.astype(F32).reshape(1), width)
    places = jnp.asarray(place_table(length, width))
    up_low, down_low = up_weight.astype(BF16), down_weight.astype(BF16)
    padded = -(-vocab // 128) * 128
    table = jnp.pad(embed, ((0, padded - vocab), (0, 0)))
    upper = table.astype(BF16)
    rest = table - upper.astype(F32)
    middle = rest.astype(BF16)
    lower = (rest - middle.astype(F32)).astype(BF16)
    embed3 = jnp.concatenate([upper, middle, lower], axis=1)
    pad_row = jnp.where(jnp.arange(padded) < vocab, 0.0, MASKED).astype(F32)[None]

    out_t, proj_t = out_weight.T, proj_weight.T
    shard = jnp.stack(
        [
            jnp.concatenate([qkv_weight[0], qkv_weight[1]], axis=1),
            jnp.concatenate([qkv_weight[2], out_t], axis=1),
            fc_weight[:, :hidden],
            fc_weight[:, hidden:],
            proj_t[:, :hidden],
            proj_t[:, hidden:],
        ]
    ).astype(BF16)
    if fused:
        source = shard
    else:
        source = lax.all_gather(lax.all_gather(shard, "dp", axis=1, tiled=True), "mp", axis=1)
        local_counts = lax.psum(local_counts, "dp")
    count_in = jnp.zeros((8, 128), F32).at[0, :NB].set(local_counts)
    whole, count_out, start, noisy, *kept = run_forward(
        fused, source, count_in, tokens[:, None], segments[:, None], segments[None], row_noise, embed3, up_low, norm_params, places, time_row, mix
    )
    if not fused:
        whole = source
    counts = count_out[0, :NB]
    live_total = jnp.sum(counts)
    bucket_weight = live_total / (NB * jnp.maximum(counts, 1.0))
    weight_total = jnp.sum(counts * bucket_weight)
    scale = my(live) * jnp.sum(my(hot) * bucket_weight, axis=-1)
    columns = jnp.stack([tokens.astype(F32), scale, scale / weight_total], axis=1)
    blocks, small, loss = run_backward(fused, whole, columns, start, noisy, kept, upper, pad_row, up_low, down_low, norm_params, mix)
    if fused:
        squares, loss_sum = loss[0, 0], loss[1, 0]
    else:
        blocks = lax.psum_scatter(blocks.astype(F32), "mp", scatter_dimension=1, tiled=False)
        blocks = lax.psum_scatter(blocks, "dp", scatter_dimension=1, tiled=True)
        small, loss_sum = lax.psum((small, loss[0, 0]), ("dp", "mp"))
        squares = lax.psum(jnp.sum(blocks * blocks), ("dp", "mp")) + jnp.sum(small * small)
    grad_norm = jnp.sqrt(squares)
    factor = jnp.minimum(1.0, CLIP_NORM / (grad_norm + 1e-06))
    grad_down = small[:, :width].T
    grad_up = small[:, width : 2 * width]
    grad_embed = small[:, 2 * width : 2 * width + vocab].T
    grad_norms = small[: 6 * width // emb, 2 * width + padded :].reshape(6, width)
    grad_qkv = jnp.stack([blocks[0][:, :half], blocks[0][:, half:], blocks[1][:, :half]])
    grad_out = blocks[1][:, half:].T
    grad_fc = jnp.concatenate([blocks[2], blocks[3]], axis=1)
    grad_proj = jnp.concatenate([blocks[4], blocks[5]], axis=1).T
    results = [loss_sum, weight_total, grad_norm]
    for weight, grad, first, second, rate, decay in (
        (embed, grad_embed, embed_m, embed_v, MATRIX_RATE, WEIGHT_DECAY),
        (up_weight, grad_up, up_m, up_v, MATRIX_RATE, WEIGHT_DECAY),
        (down_weight, grad_down, down_m, down_v, MATRIX_RATE, WEIGHT_DECAY),
        (qkv_weight, grad_qkv, qkv_m, qkv_v, MATRIX_RATE, WEIGHT_DECAY),
        (out_weight, grad_out, out_m, out_v, MATRIX_RATE, WEIGHT_DECAY),
        (fc_weight, grad_fc, fc_m, fc_v, MATRIX_RATE, WEIGHT_DECAY),
        (proj_weight, grad_proj, proj_m, proj_v, MATRIX_RATE, WEIGHT_DECAY),
        (norm_params, grad_norms, norm_m, norm_v, NORM_RATE, 0.0),
    ):
        results.extend(adam_update(weight, factor * grad, first, second, rate, decay))
    return tuple(results)


def solution(mesh):
    fused = mesh.shape["dp"] == 16 and mesh.shape["mp"] == 2
    state = {"copied": P(), "qkv": P(None, "dp", "mp"), "tall": P("mp", "dp"), "wide": P("dp", "mp")}
    kinds = ["copied"] * 3 + ["qkv", "tall", "wide", "tall", "copied"]
    weights = [state[kind] for kind in kinds]
    moments = [state[kind] for kind in kinds for unused in range(2)]
    placed = (
        P("dp", None), P("dp", None), P("dp"), P("dp", None, None), P("dp", None), P("dp", None),
        *weights,
        *moments,
    )
    outs = (P(), P(), P()) + tuple(state[kind] for kind in kinds for unused in range(3))
    return jax.shard_map(
        functools.partial(per_device, fused), mesh=mesh, in_specs=placed, out_specs=outs, check_vma=False
    )
```

time: 1390 us -> 384 us (0.28)
  waiting for transfers between devices: 674 us -> 0 us
  Pallas kernels: 0 us -> 331 us
  matrix products: 238 us -> 0 us
  blocking collectives: 209 us -> 0 us
  other arithmetic: 167 us -> 23.2 us
  local copies, waits for them, and re-layouts: 58.7 us -> 19.5 us
  between operations: 28.3 us -> 3.94 us
    reduce_scatter x11 -> x0, waiting for transfers between devices: 377 us -> none  [the longest x1 141 us: per_device(): lax.psum_scatter(layer_total[2], 'dp', scatter_dimension=0, tiled=True)]
    pallas_call x0 -> x2, Pallas kernels: none -> 331 us  [the longest x1 211 us: run_backward(): pl.pallas_call(functools.partial(backward_kernel, fused, (length, width,...]
    dot_general x68 -> x0, matrix products: 238 us -> none  [the longest x12 38.6 us: product_tn(): lax.dot_general(left, right, (((0,), (0,)), ((), ())), preferred_element_...]
    all_gather x11 -> x0, waiting for transfers between devices: 162 us -> none  [the longest x1 61.6 us: per_device(): lax.all_gather(fc_local, 'dp', axis=0, tiled=True)]
    psum x3 -> x0, blocking collectives: 159 us -> none  [the longest x1 77.9 us: per_device(): lax.psum((small_total[0], small_total[1], small_total[2], small_total[3],...]
    unnamed x24 -> x0, waiting for transfers between devices: 136 us -> none
    reduce_sum x36 -> x2, other arithmetic: 92.1 us -> 0.22 us  [the longest x1 0.13 us: per_device(): local_counts = jnp.sum(live[..., None] * hot, axis=(0, 1))]
    convert_element_type x18 -> x5, other arithmetic: 52.4 us -> 2.19 us  [the longest x2 1.4 us: per_device(): up_low, down_low = (up_weight.astype(BF16), down_weight.astype(BF16))]
  transfers between devices with their start and end apart: 23 -> 0, of which waited for: 15 -> 0; matrix products, arithmetic and copies ran while one was open for 14% -> 0% of each run, Pallas kernels for 0% -> 0%
where the time goes in v1:
time: 384 us; the launch traced here: 378 us
  Pallas kernels  331 us (86%)
  other arithmetic  23.2 us (6%)
  local copies, waits for them, and re-layouts  19.5 us (5%)
  between operations  3.94 us (1%)
    pallas_call x1, Pallas kernels, run_backward(): pl.pallas_call(functools.partial(backward_kernel, fused, (length, width,...  211 us
    pallas_call x1, Pallas kernels, run_forward(): pl.pallas_call(functools.partial(forward_kernel, fused, (length, width, p...  120 us
    unnamed x77, local copies, waits for them, and re-layouts  10.2 us
    sub x8, other arithmetic, adam_update(): weight - rate * (first_hat / (jnp.sqrt(second_hat) + ADAM_EPS) + decay *...  9.84 us

profile of v1, /device:TPU:0, one launch (start us, length us, event | category | flops | bytes accessed | tf_op | source)
XLA Modules:
  0.0 378.0 jit_solution(15676490148086029464)
XLA Ops:
  0.7 1.4 dynamic_slice.26
  4.1 0.7 fusion.34
  4.8 1.1 copy.109.refs_3_
  5.9 1.1 copy.108.refs_2_
  7.0 0.9 convert.35
  11.8 0.8 dynamic-slice_bitcast_fusion.refs_5_
  12.8 0.9 pad_maximum_fusion.refs_6_
  13.8 0.7 convert_element_type.53.refs_7_.refs_17_
  15.2 119.9 %forward.1 = (bf16[6,2,768,768]{3,2,1,0:T(8,128)(2,1)}, f32[8,128]{1,0:T(8,128)}, f32[1024,128]{1,0:T(8,128)}, bf16[1024,128]{1,0:T(8,128)(2,1)}, f32[1024,768]{...) custom-call(bf16[6,48,768]{2,1,0:T(8,128)(2,1)} %fusion.12.refs_0_, ...), custom_call_target="tpu_custom_call" | custom-call | tf_op jit(solution)/shard_map/forward/pallas_call | solution.py:694
  135.1 1.3 slice_reduce_fusion
  136.4 1.3 divide_bitcast_fusion
  137.9 1.9 fusion.23
  140.5 1.0 copy.110.refs_1_
  142.8 211.3 %backward.1 = (f32[6,48,768]{2,1,0:T(8,128)}, f32[128,2560]{1,0:T(8,128)}, f32[8,128]{1,0:T(8,128)}, bf16[6,768,768]{2,1,0:T(8,128)(2,1)}, bf16[1,256,640]{2,1,0:T(8,128)(2,1)}) custom-call(bf16[6,2,768,768]{3,2,1,0:T(8,128)(2,1)} %get-tuple-element.57.refs_0_, f32[1024,3]{1,0:T(8,128)} %copy.110.refs_1_, f32[1024,128]{1,0:T(8,128)} %get-tuple-element.59.refs_2_, ...), custom_call_target="tpu_custom_call" | custom-call | tf_op jit(solution)/shard_map/backward/pallas_call | solution.py:1159
  354.2 1.3 fusion.35
  356.2 0.7 slice_multiply_fusion.4
  357.6 1.4 slice_bitcast_fusion.1
  359.0 1.1 multiply_subtract_fusion.3
  360.1 1.1 multiply_subtract_fusion.4
  361.2 0.7 multiply_subtract_fusion.6
  362.0 0.9 multiply_subtract_fusion.5
  363.4 1.3 multiply_subtract_fusion.1
  364.8 0.9 copy.122
  365.7 0.9 copy.123
  366.6 0.9 copy.124
  367.6 2.3 multiply_subtract_fusion.2
  370.1 1.0 copy.112
  371.1 1.0 copy.114
  372.0 1.8 multiply_subtract_fusion
  373.8 0.9 copy.119
  374.7 0.9 copy.120
  375.7 0.9 copy.121
  (94 shorter events, 9.5 us)
Async XLA Ops:
  0.7 11.2 %copy-start = (f32[2,1024,128]{2,1,0:T(8,128)S(1)}, f32[2,1024,128]{2,1,0:T(8,128)}, u32[]{:S(2)}) copy-start(f32[2,1024,128]{2,1,0:T(8,128)} %param.36) | copy-start | bytes 3145732
  0.7 7.9 %copy-start.20 = (f32[384,48]{0,1:T(8,128)S(1)}, f32[384,48]{0,1:T(8,128)}, u32[]{:S(2)}) copy-start(f32[384,48]{0,1:T(8,128)} %param.43) | copy-start | bytes 221188
  0.7 8.6 %copy-start.7 = (f32[48,1536]{1,0:T(8,128)S(1)}, f32[48,1536]{1,0:T(8,128)}, u32[]{:S(2)}) copy-start(f32[48,1536]{1,0:T(8,128)} %param.44) | copy-start | bytes 884740
  0.7 9.8 %copy-start.6 = (f32[1536,48]{0,1:T(8,128)S(1)}, f32[1536,48]{0,1:T(8,128)}, u32[]{:S(2)}) copy-start(f32[1536,48]{0,1:T(8,128)} %param.45) | copy-start | bytes 884740
  4.8 5.7 %copy-start.26 = (s32[1,1024]{1,0:T(1,128)}, s32[1,1024]{1,0:T(1,128)S(1)}, u32[]{:S(2)}) copy-start(s32[1,1024]{1,0:T(1,128)S(1)} %get-tuple-element.226.refs_4_) | copy-start | bytes 12292
  7.9 4.7 %copy-start.2 = (f32[821,128]{1,0:T(8,128)S(1)}, f32[821,128]{1,0:T(8,128)}, u32[]{:S(2)}) copy-start(f32[821,128]{1,0:T(8,128)} %param.39) | copy-start | bytes 1261060
  12.7 1.1 copy-start.5
  12.7 1.8 copy-start.30
  12.7 1.8 copy-start.27
  12.8 122.3 %copy-start.3 = (bf16[896,128]{1,0:T(8,128)(2,1)}, bf16[896,128]{1,0:T(8,128)(2,1)S(1)}, u32[]{:S(2)}) copy-start(bf16[896,128]{1,0:T(8,128)(2,1)S(1)} %pad_convert_fusion.refs_15_) | copy-start | bytes 688132
  15.2 126.3 %copy-start.4 = (f32[768,128]{1,0:T(8,128)S(1)}, f32[768,128]{1,0:T(8,128)}, u32[]{:S(2)}) copy-start(f32[768,128]{1,0:T(8,128)} %param.41) | copy-start | bytes 1179652
  142.8 214.1 %copy-start.21 = (f32[6,768]{1,0:T(8,128)S(1)}, f32[6,768]{1,0:T(8,128)}, u32[]{:S(2)}) copy-start(f32[6,768]{1,0:T(8,128)} %refs_19_.1) | copy-start | bytes 55300
  142.8 214.1 %copy-start.28 = (f32[6,768]{1,0:T(8,128)S(1)}, f32[6,768]{1,0:T(8,128)}, u32[]{:S(2)}) copy-start(f32[6,768]{1,0:T(8,128)} %param.62) | copy-start | bytes 55300
  142.8 214.1 %copy-start.29 = (f32[6,768]{1,0:T(8,128)S(1)}, f32[6,768]{1,0:T(8,128)}, u32[]{:S(2)}) copy-start(f32[6,768]{1,0:T(8,128)} %param.61) | copy-start | bytes 55300
  354.2 4.8 %copy-start.16 = (f32[1536,48]{0,1:T(8,128)S(1)}, f32[1536,48]{0,1:T(8,128)}, u32[]{:S(2)}) copy-start(f32[1536,48]{0,1:T(8,128)} %param.60) | copy-start | bytes 884740
  354.2 4.8 %copy-start.17 = (f32[1536,48]{0,1:T(8,128)S(1)}, f32[1536,48]{0,1:T(8,128)}, u32[]{:S(2)}) copy-start(f32[1536,48]{0,1:T(8,128)} %param.59) | copy-start | bytes 884740
  357.6 2.5 copy-start.8
  357.6 2.5 copy-start.18
  357.6 2.5 copy-start.19
  359.0 2.2 copy-start.24
  359.0 2.2 copy-start.25
  360.1 1.9 copy-start.9
  360.1 1.9 copy-start.22
  360.1 1.9 copy-start.23
  361.2 1.7 copy-start.12
  361.2 1.9 copy-start.13
  364.8 2.8 copy-start.14
  364.8 2.8 copy-start.15
  367.5 2.3 copy-start.10
  367.5 2.5 copy-start.11
  372.0 4.6 %copy-start.1 = (f32[2,1024,128]{2,1,0:T(8,128)S(1)}, f32[2,1024,128]{2,1,0:T(8,128)}, u32[]{:S(2)}) copy-start(f32[2,1024,128]{2,1,0:T(8,128)} %param.36) | copy-start | bytes 3145732
